TPU v7x, 256 devices: a whole 4x4x8 slice. The times are simulated.
256 devices in a mesh: cfg: 2 (over core), fsdp: 8 (over x_hi, y), seq: 16 (over x_lo, z).
Axes of the slice: x: 4 (x_hi: 2, x_lo: 2; x = x_hi * 2 + x_lo), y: 4, z: 8, core: 2. Of those that a mesh axis runs over, the one named last changes fastest.
Arguments:
- query_act: bfloat16 [2, 8, 2048, 2048], P('cfg', 'fsdp', 'seq'), may hold values from -24 to 24
- key_act: bfloat16 [2, 8, 2048, 2048], P('cfg', 'fsdp', 'seq'), may hold values from -4 to 4
- value_act: bfloat16 [2, 8, 2048, 2048], P('cfg', 'fsdp', 'seq'), may hold values from -6 to 6
- out_weight: bfloat16 [2048, 1536], P(('fsdp', 'seq')), may hold values from -0.125 to 0.125
- reward_dir: bfloat16 [8, 2048, 1536], P('fsdp', 'seq'), may hold values from -6 to 6
- guide_index: int32 [1], replicated, may hold values from 0 to 127
- step_index: int32 [1], replicated, may hold values from 0 to 49
Outputs:
- guided: bfloat16 [8, 2048, 1536], P('fsdp', 'seq')
- grad_query: bfloat16 [2, 8, 2048, 2048], P('cfg', 'fsdp', 'seq')
- grad_key: bfloat16 [2, 8, 2048, 2048], P('cfg', 'fsdp', 'seq')
- grad_value: bfloat16 [2, 8, 2048, 2048], P('cfg', 'fsdp', 'seq')
- grad_weight: float32 [2048, 1536], P(('fsdp', 'seq'))
All inputs are finite; a program needn't handle non-finite values.
Results may differ from a plain program's by a relative error of at most 0.01.
Values may be sent and summed in bfloat16 or wider, within the bound.
No kernel may reach another device: no remote copies, remote signals or barrier semaphores. Data moves between devices by JAX's collectives and lax.ppermute only.
A program may use at most 128 MiB of HBM per device.

v0:
```python
import jax
import jax.numpy as jnp
from jax import lax
from jax.sharding import PartitionSpec as P

HDIM = 128
STEPS = 50


GUIDE_STEP = 0.04


def swapped(value, axis, distance):
    mask = 2**distance
    pairs = [(source, source ^ mask) for source in range(lax.axis_size(axis))]
    return lax.ppermute(value, axis, pairs)


def split_heads(array):
    return array.reshape(array.shape[:3] + (array.shape[3] // HDIM, HDIM))


def to_blocks(array, count, block):
    shape = array.shape
    return jnp.moveaxis(array.reshape(shape[:2] + (count, block) + shape[3:]), 2, 0)


def from_blocks(array):
    moved = jnp.moveaxis(array, 0, 2)
    shape = moved.shape
    return moved.reshape(shape[:2] + (shape[2] * shape[3],) + shape[4:])


def stats_blocks(array, count, block):
    shape = array.shape
    return jnp.moveaxis(array.reshape(shape[:3] + (count, block)), 3, 0)


def stats_whole(array):
    moved = jnp.moveaxis(array, 0, 3)
    shape = moved.shape
    return moved.reshape(shape[:3] + (shape[3] * shape[4],))


def attend_forward(pack):
    query_h, key_h, value_h = pack
    factor = HDIM ** (-0.5)
    queries, keys_all, values_all = (split_heads(query_h), split_heads(key_h), split_heads(value_h))
    length = queries.shape[2]
    block = min(512, length)
    count = length // block

    def one_block(query_part):
        scores = (
            jnp.einsum(
                "bsqhd,bskhd->bshqk", query_part, keys_all, preferred_element_type=jnp.float32
            )
            * factor
        )
        peak = jnp.max(scores, axis=-1)
        weights = jnp.exp(scores - peak[..., None])
        total = jnp.sum(weights, axis=-1)
        probs = (weights / total[..., None]).astype(jnp.bfloat16)
        mixed = jnp.einsum(
            "bshqk,bskhd->bsqhd", probs, values_all, preferred_element_type=jnp.float32
        )
        return (mixed.astype(jnp.bfloat16), peak, total)

    mixed, peak, total = lax.map(one_block, to_blocks(queries, count, block))
    mixed = from_blocks(mixed)
    mixed = mixed.reshape(mixed.shape[:3] + (mixed.shape[3] * HDIM,))
    return (mixed, stats_whole(peak), stats_whole(total), query_h, key_h, value_h)


def attend_backward(grad_h, query_h, key_h, value_h, mixed_h, peak, total):
    factor = HDIM ** (-0.5)
    queries, keys_all, values_all = (split_heads(query_h), split_heads(key_h), split_heads(value_h))
    grads, outputs = (split_heads(grad_h), split_heads(mixed_h))
    length = queries.shape[2]
    block = min(512, length)
    count = length // block
    parts = (
        to_blocks(queries, count, block),
        to_blocks(grads, count, block),
        to_blocks(outputs, count, block),
        stats_blocks(peak, count, block),
        stats_blocks(total, count, block),
    )

    def step(carry, part):
        dkey_acc, dvalue_acc = carry
        query_part, grad_part, out_part, peak_part, total_part = part
        scores = (
            jnp.einsum(
                "bsqhd,bskhd->bshqk", query_part, keys_all, preferred_element_type=jnp.float32
            )
            * factor
        )
        probs = jnp.exp(scores - peak_part[..., None]) / total_part[..., None]
        rounded = probs.astype(jnp.bfloat16)
        dvalue_acc = dvalue_acc + jnp.einsum(
            "bshqk,bsqhd->bskhd", rounded, grad_part, preferred_element_type=jnp.float32
        )
        dprobs = jnp.einsum(
            "bsqhd,bskhd->bshqk", grad_part, values_all, preferred_element_type=jnp.float32
        )
        inner = jnp.sum(grad_part.astype(jnp.float32) * out_part.astype(jnp.float32), axis=-1)
        inner = jnp.moveaxis(inner, 3, 2)
        dscores = (probs * (dprobs - inner[..., None])).astype(jnp.bfloat16)
        dquery = (
            jnp.einsum("bshqk,bskhd->bsqhd", dscores, keys_all, preferred_element_type=jnp.float32)
            * factor
        )
        dkey_acc = (
            dkey_acc
            + jnp.einsum(
                "bshqk,bsqhd->bskhd", dscores, query_part, preferred_element_type=jnp.float32
            )
            * factor
        )
        return ((dkey_acc, dvalue_acc), dquery.astype(jnp.bfloat16))

    start = (jnp.zeros(keys_all.shape, jnp.float32), jnp.zeros(keys_all.shape, jnp.float32))
    (dkey_acc, dvalue_acc), dquery = lax.scan(step, start, parts)
    dquery = from_blocks(dquery)
    shape = query_h.shape
    return (
        dquery.reshape(shape),
        dkey_acc.astype(jnp.bfloat16).reshape(shape),
        dvalue_acc.astype(jnp.bfloat16).reshape(shape),
    )


def local(query_act, key_act, value_act, out_weight, reward_dir, guide_index, step_index):
    mixed_h, peak, total, query_h, key_h, value_h = attend_forward(
        (
            lax.all_to_all(query_act, "seq", split_axis=3, concat_axis=2, tiled=True),
            lax.all_to_all(key_act, "seq", split_axis=3, concat_axis=2, tiled=True),
            lax.all_to_all(value_act, "seq", split_axis=3, concat_axis=2, tiled=True),
        )
    )
    mixed_tok = lax.all_to_all(mixed_h, "seq", split_axis=2, concat_axis=3, tiled=True)
    flat = mixed_tok[0, 0]
    moment = step_index[0].astype(jnp.float32)
    gate = jnp.cos(0.5 * jnp.pi * (moment + 0.5) / STEPS)
    strength = 1.0 + GUIDE_STEP * guide_index[0].astype(jnp.float32)
    columns = flat
    proj = jnp.dot(
        columns,
        lax.all_gather(out_weight, ("fsdp", "seq"), axis=0, tiled=True),
        preferred_element_type=jnp.float32,
    )
    branch_out = (gate * proj).astype(jnp.bfloat16)
    partner_out = swapped(branch_out, "cfg", 0)
    is_cond = lax.axis_index("cfg") == 0
    cond = jnp.where(is_cond, branch_out, partner_out).astype(jnp.float32)
    uncond = jnp.where(is_cond, partner_out, branch_out).astype(jnp.float32)
    guided = uncond + strength * (cond - uncond)
    resid = reward_dir[0].astype(jnp.float32) - guided
    coeff = jnp.where(is_cond, strength, 1.0 - strength)
    grad_out = (gate * coeff * resid).astype(jnp.bfloat16)
    grad_mixed = lax.dot_general(
        grad_out,
        lax.all_gather(out_weight, ("fsdp", "seq"), axis=0, tiled=True),
        (((1,), (1,)), ((), ())),
        preferred_element_type=jnp.float32,
    )
    grad_mixed = grad_mixed.astype(jnp.bfloat16)[None, None]
    grad_h = lax.all_to_all(grad_mixed, "seq", split_axis=3, concat_axis=2, tiled=True)
    dquery_h, dkey_h, dvalue_h = attend_backward(
        grad_h, query_h, key_h, value_h, mixed_h, peak, total
    )
    grad_query, grad_key, grad_value = (
        lax.all_to_all(dquery_h, "seq", split_axis=2, concat_axis=3, tiled=True),
        lax.all_to_all(dkey_h, "seq", split_axis=2, concat_axis=3, tiled=True),
        lax.all_to_all(dvalue_h, "seq", split_axis=2, concat_axis=3, tiled=True),
    )
    columns = flat
    partial_grad = lax.psum_scatter(
        lax.dot_general(
            columns, grad_out, (((0,), (0,)), ((), ())), preferred_element_type=jnp.float32
        ),
        ("fsdp", "seq"),
        scatter_dimension=0,
        tiled=True,
    )
    grad_weight = lax.psum(partial_grad.astype(jnp.bfloat16), "cfg").astype(jnp.float32)
    return (guided.astype(jnp.bfloat16)[None], grad_query, grad_key, grad_value, grad_weight)


def solution(mesh):
    placed = (
        P("cfg", "fsdp", "seq", None),
        P("cfg", "fsdp", "seq", None),
        P("cfg", "fsdp", "seq", None),
        P(("fsdp", "seq"), None),
        P("fsdp", "seq", None),
        P(),
        P(),
    )
    return jax.shard_map(
        local,
        mesh=mesh,
        in_specs=placed,
        out_specs=(
            P("fsdp", "seq", None),
            P("cfg", "fsdp", "seq", None),
            P("cfg", "fsdp", "seq", None),
            P("cfg", "fsdp", "seq", None),
            P(("fsdp", "seq"), None),
        ),
        check_vma=False,
    )
```

profile of v0, /device:TPU:1, one launch (start us, length us, event | category | flops | bytes accessed | tf_op | source)
XLA Modules:
  0.0 1432.7 jit_solution(17263568205966993945)
XLA Ops:
  10.9 11.6 reduce.6
  23.4 10.0 all-to-all-start
  34.2 11.6 reduce.7
  56.5 11.6 reduce.8
  78.8 13.5 all-to-all-done.2
  93.3 10.8 while.29
  104.1 8.1 copy.116
  112.3 12.8 reduce.9
  127.1 5.7 all-to-all-start.3
  133.6 13.5 all-to-all-done.3
  151.5 441.3 %all-gather.2.cloned.1.call-done = bf16[2048,1536]{1,0:T(8,128)(2,1)} async-done(((bf16[16,1536]{1,0:T(8,128)(2,1)}), bf16[2048,1536]{1,0:T(8,128)(2,1)}) %all-gather.2.cloned.1.call-update) | async-done | bytes 6291472 | tf_op jit(solution)/shard_map/all_gather | solution.py:150
  596.6 91.0 %collective-permute-start = (bf16[128,1536]{1,0:T(8,128)(2,1)S(1)}, bf16[128,1536]{1,0:T(8,128)(2,1)S(1)}, u32[]{:S(2)}, u32[]{:S(2)}) collective-permute-start(bf16[128,1536]{1,0:T(8,128)(2,1)S(1)} %fusion.34), channel_id=1, source_target_pairs={{0,128},{128,0},{1,129},{129,1},{2,130},{130,2},{3,131},{131,3},{4... | collective-permute-start | bytes 1179656 | tf_op jit(solution)/shard_map/ppermute | solution.py:16
  690.0 6.3 fusion.41
  702.2 11.6 reduce.10
  719.0 19.4 %all-to-all-done.4 = bf16[16,2,8192]{2,1,0:T(2,128)(2,1)} async-done(((bf16[16,2,8192]{2,1,0:T(2,128)(2,1)}), bf16[16,2,8192]{2,1,0:T(2,128)(2,1)}, u32[]{:S(2)}, u32[]{:S(2)}) %all-to-all-start.4) | async-done | bytes 524320 | tf_op jit(solution)/shard_map/all_to_all | solution.py:169
  746.9 29.2 %while.30 = (s32[]{:T(128)}, f32[1,1,2048,1,128]{2,4,3,1,0:T(8,128)S(1)}, f32[1,1,2048,1,128]{2,4,3,1,0:T(8,128)S(1)}, bf16[4,1,1,512,1,128]{5,3,4,2,1,0:T(8,128...) while((s32[]{:T(128)}, ...), condition=%wide.region_6.7_spmd.clone, body=%wide.region_4.6_spmd.clone.sunk | while | flops 1351220736 | bytes 27672776 | solution.py:124
  777.9 12.4 reduce.11
  799.4 11.6 reduce.12
  819.8 8.1 copy.113
  828.0 11.6 reduce.13
  840.5 7.6 all-to-all-start.7
  853.6 8.9 all-to-all-done.7
  864.3 458.4 %reduce-scatter.2.cloned.1.call-done = f32[16,1536]{1,0:T(8,128)} async-done(((f32[2048,1536]{1,0:T(8,128)}), f32[16,1536]{1,0:T(8,128)}) %reduce-scatter.2.cloned.1.call-update) | async-done | bytes 98320 | tf_op jit(solution)/shard_map/reduce_scatter | solution.py:179
  1323.6 101.2 %psum.7 = bf16[16,1536]{1,0:T(8,128)(2,1)S(1)} all-reduce(bf16[16,1536]{1,0:T(8,128)(2,1)S(1)} %convert_element_type.116), channel_id=1, replica_groups=mesh['cfg'=2,'fsdp'=8,'seq'=16] {'cfg'}, use_global_device_ids=true, to_apply=%region_8.9 | all-reduce | flops 24576 | bytes 98304 | tf_op jit(solution)/shard_map/psum | solution.py:187
  (131 shorter events, 128.3 us)
Async XLA Ops:
  7.2 26.3 %copy-start.3 = (bf16[1,1,128,2048]{3,2,1,0:T(8,128)(2,1)S(1)}, bf16[1,1,128,2048]{3,2,1,0:T(8,128)(2,1)}, u32[]{:S(2)}) copy-start(bf16[1,1,128,2048]{3,2,1,0:T(8,128)(2,1)} %param.12) | copy-start | bytes 1572868
  7.2 585.6 %all-gather.2.cloned.1.call-start = ((), (), s32[]{:S(2)}) async-start(), calls=%async_computation.9 | async-start | bytes 6340608 | tf_op jit(solution)/shard_map/all_gather | solution.py:150
  10.9 44.8 %copy-start.4 = (bf16[1,1,128,2048]{3,2,1,0:T(8,128)(2,1)S(1)}, bf16[1,1,128,2048]{3,2,1,0:T(8,128)(2,1)}, u32[]{:S(2)}) copy-start(bf16[1,1,128,2048]{3,2,1,0:T(8,128)(2,1)} %param.13) | copy-start | bytes 1572868
  23.4 26.6 %all-to-all-start = ((bf16[16,2,8192]{2,1,0:T(2,128)(2,1)}), bf16[16,2,8192]{2,1,0:T(2,128)(2,1)S(1)}, u32[]{:S(2)}, u32[]{:S(2)}) async-start(bf16[16,2,8192]{2,1,0:T(2,128)(2,1)} %reshape.170), calls=%async_computation | async-start | bytes 1048576 | tf_op jit(solution)/shard_map/all_to_all | solution.py:137
  50.0 21.6 %all-to-all-start.1 = ((bf16[16,2,8192]{2,1,0:T(2,128)(2,1)}), bf16[16,2,8192]{2,1,0:T(2,128)(2,1)S(1)}, u32[]{:S(2)}, u32[]{:S(2)}) async-start(bf16[16,2,8192]{2,1,0:T(2,128)(2,1)} %reshape.172), calls=%async_computation.1 | async-start | bytes 1048576 | tf_op jit(solution)/shard_map/all_to_all | solution.py:138
  71.6 20.7 %all-to-all-start.2 = ((bf16[16,2,8192]{2,1,0:T(2,128)(2,1)}), bf16[16,2,8192]{2,1,0:T(2,128)(2,1)S(1)}, u32[]{:S(2)}, u32[]{:S(2)}) async-start(bf16[16,2,8192]{2,1,0:T(2,128)(2,1)} %reshape.174), calls=%async_computation.2 | async-start | bytes 1048576 | tf_op jit(solution)/shard_map/all_to_all | solution.py:139
  104.1 46.0 %copy-start.1 = (bf16[4,1,1,512,1,128]{5,3,4,2,1,0:T(8,128)(2,1)}, bf16[4,1,1,512,1,128]{5,3,4,2,1,0:T(8,128)(2,1)S(1)}, u32[]{:S(2)}) copy-start(bf16[4,1,1,512,1,128]{5,3,4,2,1,0:T(8,128)(2,1)S(1)} %get-tuple-element.502) | copy-start | bytes 1572868
  104.1 46.0 %copy-start.2 = (bf16[4,1,1,512,1,128]{5,3,4,2,1,0:T(8,128)(2,1)}, bf16[4,1,1,512,1,128]{5,3,4,2,1,0:T(8,128)(2,1)S(1)}, u32[]{:S(2)}) copy-start(bf16[4,1,1,512,1,128]{5,3,4,2,1,0:T(8,128)(2,1)S(1)} %get-tuple-element.466) | copy-start | bytes 1572868
  127.1 20.0 %all-to-all-start.3 = ((bf16[16,2,8192]{2,1,0:T(2,128)(2,1)}), bf16[16,2,8192]{2,1,0:T(2,128)(2,1)}, u32[]{:S(2)}, u32[]{:S(2)}) async-start(bf16[16,2,8192]{2,1,0:T(2,128)(2,1)} %reshape.176), calls=%async_computation.3 | async-start | bytes 1048576 | tf_op jit(solution)/shard_map/all_to_all | solution.py:142
  132.8 1189.9 %reduce-scatter.2.cloned.1.call-start = ((), (), s32[]{:S(2)}) async-start(), calls=%async_computation.10 | async-start | bytes 12681216 | tf_op jit(solution)/shard_map/reduce_scatter | solution.py:179
  150.2 538.8 %copy-start.5 = (bf16[1,128,1536]{2,1,0:T(8,128)(2,1)S(1)}, bf16[1,128,1536]{2,1,0:T(8,128)(2,1)}, u32[]{:S(2)}) copy-start(bf16[1,128,1536]{2,1,0:T(8,128)(2,1)} %param.15) | copy-start | bytes 1179652
  596.6 92.3 %collective-permute-start = (bf16[128,1536]{1,0:T(8,128)(2,1)S(1)}, bf16[128,1536]{1,0:T(8,128)(2,1)S(1)}, u32[]{:S(2)}, u32[]{:S(2)}) collective-permute-start(bf16[128,1536]{1,0:T(8,128)(2,1)S(1)} %fusion.34), channel_id=1, source_target_pairs={{0,128},{128,0},{1,129},{129,1},{2,130},{130,2},{3,131},{131,3},{4... | collective-permute-start | bytes 1179656 | tf_op jit(solution)/shard_map/ppermute | solution.py:16
  714.7 23.7 %all-to-all-start.4 = ((bf16[16,2,8192]{2,1,0:T(2,128)(2,1)}), bf16[16,2,8192]{2,1,0:T(2,128)(2,1)}, u32[]{:S(2)}, u32[]{:S(2)}) async-start(bf16[16,2,8192]{2,1,0:T(2,128)(2,1)} %reshape.178), calls=%async_computation.4 | async-start | bytes 1048576 | tf_op jit(solution)/shard_map/all_to_all | solution.py:169
  748.0 2.0 copy-start
  755.3 2.0 copy-start
  762.6 2.0 copy-start
  769.9 2.0 copy-start
  792.2 21.9 %all-to-all-start.5 = ((bf16[16,2,8192]{2,1,0:T(2,128)(2,1)}), bf16[16,2,8192]{2,1,0:T(2,128)(2,1)}, u32[]{:S(2)}, u32[]{:S(2)}) async-start(bf16[16,2,8192]{2,1,0:T(2,128)(2,1)} %reshape.180), calls=%async_computation.5 | async-start | bytes 1048576 | tf_op jit(solution)/shard_map/all_to_all | solution.py:174
  814.1 26.4 %all-to-all-start.6 = ((bf16[16,2,8192]{2,1,0:T(2,128)(2,1)}), bf16[16,2,8192]{2,1,0:T(2,128)(2,1)S(1)}, u32[]{:S(2)}, u32[]{:S(2)}) async-start(bf16[16,2,8192]{2,1,0:T(2,128)(2,1)} %reshape.182), calls=%async_computation.6 | async-start | bytes 1048576 | tf_op jit(solution)/shard_map/all_to_all | solution.py:175
  840.5 21.9 %all-to-all-start.7 = ((bf16[16,2,8192]{2,1,0:T(2,128)(2,1)}), bf16[16,2,8192]{2,1,0:T(2,128)(2,1)S(1)}, u32[]{:S(2)}, u32[]{:S(2)}) async-start(bf16[16,2,8192]{2,1,0:T(2,128)(2,1)} %reshape.184), calls=%async_computation.7 | async-start | bytes 1048576 | tf_op jit(solution)/shard_map/all_to_all | solution.py:176
Sparse Core Ops, SparseCore 0:
  9.8 582.9 all-gather.1
  696.5 626.1 reduce-scatter.1
where the time goes:
time: 1440 us; the launch traced here: 1430 us
  waiting for transfers between devices  964 us (67%)
  starting transfers between devices  140 us (10%)
  other arithmetic  105 us (7%)
  blocking collectives  101 us (7%)
  local copies, waits for them, and re-layouts  59.1 us (4%)
  matrix products  46.8 us (3%)
  between operations  16.2 us (1%)
    reduce_scatter x1, waiting for transfers between devices, local(): lax.psum_scatter(lax.dot_general(columns, grad_out, (((0,), (0,)), ((), (...  458 us
    all_gather x1, waiting for transfers between devices, local(): lax.all_gather(out_weight, ('fsdp', 'seq'), axis=0, tiled=True)  441 us
    psum x1, blocking collectives, local(): lax.psum(partial_grad.astype(jnp.bfloat16), 'cfg').astype(jnp.float32)  101 us
    unnamed x10, other arithmetic  94.7 us
    ppermute x1, starting transfers between devices, swapped(): return lax.ppermute(value, axis, pairs)  91 us
    unnamed x41, local copies, waits for them, and re-layouts  30.9 us
  transfers between devices with their start and end apart: 11, of which 10 were waited for; matrix products, arithmetic and copies ran while one was open for 14% of the time, Pallas kernels for 0%

commit v1 on v0

v1 whole, which is shorter than its diff:
```python
import functools

import jax
import jax.numpy as jnp
from jax import lax
from jax.experimental import pallas as pl
from jax.experimental.pallas import tpu as pltpu
from jax.sharding import PartitionSpec as P

HDIM = 128
STEPS = 50
GUIDE_STEP = 0.04
LOG2E = 1.4426950408889634
BF = jnp.bfloat16
F32 = jnp.float32
NT = (((1,), (1,)), ((), ()))
VMEM_LIMIT = 56 * 1024 * 1024


def params():
    return pltpu.CompilerParams(vmem_limit_bytes=VMEM_LIMIT)


def whole(count):
    return [pl.BlockSpec(memory_space=pltpu.VMEM) for _ in range(count)]


def pack_kernel(q_ref, k_ref, v_ref, out_ref):
    rows = q_ref.shape[0]
    for head in range(out_ref.shape[0]):
        lanes = slice(head * HDIM, (head + 1) * HDIM)
        for place, ref in enumerate((q_ref, k_ref, v_ref)):
            out_ref[head, place * rows : (place + 1) * rows, :] = ref[:, lanes]


def pack_heads(query, key, value):
    rows, width = query.shape
    return pl.pallas_call(
        pack_kernel,
        out_shape=jax.ShapeDtypeStruct((width // HDIM, 3 * rows, HDIM), BF),
        in_specs=whole(3),
        out_specs=whole(1)[0],
        compiler_params=params(),
        name="pack_heads",
    )(query, key, value)


def unpack_kernel(in_ref, q_ref, k_ref, v_ref):
    rows = q_ref.shape[0]
    for head in range(in_ref.shape[0]):
        lanes = slice(head * HDIM, (head + 1) * HDIM)
        for place, ref in enumerate((q_ref, k_ref, v_ref)):
            ref[:, lanes] = in_ref[head, place * rows : (place + 1) * rows, :]


def unpack_heads(packed):
    heads, rows3, _ = packed.shape
    shape = jax.ShapeDtypeStruct((rows3 // 3, heads * HDIM), BF)
    return pl.pallas_call(
        unpack_kernel,
        out_shape=(shape, shape, shape),
        in_specs=whole(1),
        out_specs=tuple(whole(3)),
        compiler_params=params(),
        name="unpack_heads",
    )(packed)


def forward_kernel(qkv_ref, out_ref, probs_ref, value_t):
    shards, rows3, _ = qkv_ref.shape
    rows = rows3 // 3
    length = shards * rows
    step = pl.program_id(0)
    take = out_ref.shape[0]

    @pl.when(step == 0)
    def _():
        value = qkv_ref[:, 2 * rows :, :].reshape(length, HDIM)
        value_t[...] = value.astype(F32).T.astype(BF)

    query = qkv_ref[pl.ds(step * take, take), :rows, :].reshape(take * rows, HDIM)
    keys = qkv_ref[:, rows : 2 * rows, :].reshape(length, HDIM)
    scores = lax.dot_general(keys, query, NT, preferred_element_type=F32)
    scale = HDIM ** (-0.5) * LOG2E
    peak = jnp.max(scores, axis=0, keepdims=True) * scale
    weights = jnp.exp2(scores * scale - peak)
    total = jnp.sum(weights, axis=0, keepdims=True)
    probs = (weights * (1.0 / total)).astype(BF)
    probs_ref[...] = probs
    mixed_t = jnp.dot(value_t[...], probs, preferred_element_type=F32)
    out_ref[...] = mixed_t.T.astype(BF).reshape(out_ref.shape)


def attend_forward(qkv):
    shards, rows3, _ = qkv.shape
    rows = rows3 // 3
    length = shards * rows
    take = 2
    return pl.pallas_call(
        forward_kernel,
        grid=(shards // take,),
        out_shape=(
            jax.ShapeDtypeStruct((shards, rows, HDIM), BF),
            jax.ShapeDtypeStruct((length, length), BF),
        ),
        in_specs=whole(1),
        out_specs=(
            pl.BlockSpec((take, rows, HDIM), lambda i: (i, 0, 0)),
            pl.BlockSpec((length, take * rows), lambda i: (0, i)),
        ),
        scratch_shapes=[pltpu.VMEM((HDIM, length), BF)],
        compiler_params=params(),
        name="attend_forward",
    )(qkv)


def backward_kernel(qkv_ref, mixed_ref, grad_ref, probs_ref, out_ref, inner, query_t):
    shards, rows3, _ = qkv_ref.shape
    rows = rows3 // 3
    length = shards * rows
    step = pl.program_id(0)
    block = probs_ref.shape[0]
    take = block // rows
    factor = HDIM ** (-0.5)
    grad = grad_ref[...].reshape(length, HDIM)

    @pl.when(step == 0)
    def _():
        mixed = mixed_ref[...].reshape(length, HDIM)
        product = grad.astype(F32) * mixed.astype(F32)
        inner[...] = jnp.sum(product.T, axis=0, keepdims=True)
        query_t[...] = jnp.zeros_like(query_t)

    query = qkv_ref[:, :rows, :].reshape(length, HDIM)
    here = pl.ds(step * take, take)
    keys = qkv_ref[here, rows : 2 * rows, :].reshape(block, HDIM)
    value = qkv_ref[here, 2 * rows :, :].reshape(block, HDIM)
    probs = probs_ref[...]
    grad_value = jnp.dot(probs, grad, preferred_element_type=F32)
    out_ref[here, 2 * rows :, :] = grad_value.astype(BF).reshape(take, rows, HDIM)
    grad_probs = lax.dot_general(value, grad, NT, preferred_element_type=F32)
    grad_scores = (probs.astype(F32) * (grad_probs - inner[...])).astype(BF)
    grad_key = jnp.dot(grad_scores, query, preferred_element_type=F32) * factor
    out_ref[here, rows : 2 * rows, :] = grad_key.astype(BF).reshape(take, rows, HDIM)
    keys_t = keys.astype(F32).T.astype(BF)
    query_t[...] += jnp.dot(keys_t, grad_scores, preferred_element_type=F32)

    @pl.when(step == pl.num_programs(0) - 1)
    def _():
        grad_query = (query_t[...] * factor).T.astype(BF)
        out_ref[:, :rows, :] = grad_query.reshape(shards, rows, HDIM)


def attend_backward(qkv, mixed, grad, probs):
    shards, rows3, _ = qkv.shape
    rows = rows3 // 3
    length = shards * rows
    take = 2
    return pl.pallas_call(
        backward_kernel,
        grid=(shards // take,),
        out_shape=jax.ShapeDtypeStruct(qkv.shape, BF),
        in_specs=whole(3) + [pl.BlockSpec((take * rows, length), lambda i: (i, 0))],
        out_specs=whole(1)[0],
        scratch_shapes=[pltpu.VMEM((1, length), F32), pltpu.VMEM((HDIM, length), F32)],
        compiler_params=params(),
        name="attend_backward",
    )(qkv, mixed, grad, probs)


def weight_blocks(refs):
    own, beside, left, right, far_own, far_beside = refs
    return [own[...], right[0], far_own[...], left[0], beside[...], right[1], far_beside[...], left[1]]


def columns_of(own_ref, other_ref, head):
    return jnp.concatenate(
        [
            jnp.concatenate([own_ref[head], own_ref[head + 1]], axis=1),
            jnp.concatenate([other_ref[head], other_ref[head + 1]], axis=1),
        ],
        axis=0,
    )


def project_kernel(
    place_ref, scalar_ref, own_ref, other_ref, reward_ref,
    w0, w1, w2, w3, w4, w5,
    guided_ref, grad_ref, keep_ref, send_ref,
):
    blocks = weight_blocks((w0, w1, w2, w3, w4, w5))
    rows = own_ref.shape[1]
    half = guided_ref.shape[1]
    first = place_ref[8] == 0
    gate, strength = scalar_ref[0], scalar_ref[1]
    total = None
    for place, block in enumerate(blocks):
        columns = columns_of(own_ref, other_ref, 2 * place_ref[place])
        part = jnp.dot(columns, block, preferred_element_type=F32)
        total = part if total is None else total + part
    branch_out = (gate * total).astype(BF).astype(F32)
    own_out, other_out = branch_out[:rows], branch_out[rows:]
    cond = jnp.where(first, own_out, other_out)
    uncond = jnp.where(first, other_out, own_out)
    guided = uncond + strength * (cond - uncond)
    guided_ref[...] = guided.astype(BF)
    reward = jnp.where(first, reward_ref[:, :half], reward_ref[:, half:]).astype(F32)
    resid = reward - guided
    own_coeff = gate * jnp.where(first, strength, 1.0 - strength)
    other_coeff = gate * jnp.where(first, 1.0 - strength, strength)
    grad = jnp.concatenate([own_coeff * resid, other_coeff * resid], axis=0).astype(BF)
    grad_ref[...] = grad
    for place, block in enumerate(blocks):
        head = 2 * place_ref[place]
        part = lax.dot_general(grad, block, NT, preferred_element_type=F32)
        for odd in range(2):
            lanes = part[:, odd * HDIM : (odd + 1) * HDIM]
            keep_ref[head + odd] = lanes[:rows]
            send_ref[head + odd] = lanes[rows:].astype(BF)


def project(place, scalars, own, other, reward, blocks):
    heads, rows, _ = own.shape
    half = reward.shape[1] // 2
    smem = pl.BlockSpec(memory_space=pltpu.SMEM)
    return pl.pallas_call(
        project_kernel,
        out_shape=(
            jax.ShapeDtypeStruct((rows, half), BF),
            jax.ShapeDtypeStruct((2 * rows, half), BF),
            jax.ShapeDtypeStruct((heads, rows, HDIM), F32),
            jax.ShapeDtypeStruct((heads, rows, HDIM), BF),
        ),
        in_specs=[smem, smem] + whole(3 + len(blocks)),
        out_specs=tuple(whole(4)),
        compiler_params=params(),
        name="project",
    )(place, scalars, own, other, reward, *blocks)


def weight_kernel(place_ref, own_ref, other_ref, grad_ref, here_ref, right_ref, far_ref, left_ref):
    grad = grad_ref[...]
    for place in range(8):
        columns = columns_of(own_ref, other_ref, 2 * place_ref[place])
        flipped = columns.astype(F32).T.astype(BF)
        part = jnp.dot(flipped, grad, preferred_element_type=F32)
        ref = (here_ref, right_ref, far_ref, left_ref)[place % 4]
        ref[place // 4] = part.astype(ref.dtype)


def weight_gradient(place, own, other, grad):
    shape = (2, 2 * HDIM, grad.shape[1])
    return pl.pallas_call(
        weight_kernel,
        out_shape=(
            jax.ShapeDtypeStruct(shape, F32),
            jax.ShapeDtypeStruct(shape, BF),
            jax.ShapeDtypeStruct(shape, BF),
            jax.ShapeDtypeStruct(shape, BF),
        ),
        in_specs=[pl.BlockSpec(memory_space=pltpu.SMEM)] + whole(3),
        out_specs=tuple(whole(4)),
        compiler_params=params(),
        name="weight_gradient",
    )(place, own, other, grad)


def shift_y(value, step):
    pairs = [(i, (i // 4) * 4 + (i % 4 + step) % 4) for i in range(8)]
    return lax.ppermute(value, "fsdp", pairs)


def swap(value, axis, mask):
    pairs = [(i, i ^ mask) for i in range(lax.axis_size(axis))]
    return lax.ppermute(value, axis, pairs)


SEQ_MASKS = (8, 4, 2, 1)


def gather_seq(part):
    place = lax.axis_index("seq")
    for mask in SEQ_MASKS[::-1]:
        got = swap(part, "seq", mask)
        low = (place & mask) == 0
        part = jnp.where(low, jnp.concatenate([part, got]), jnp.concatenate([got, part]))
    return part


def scatter_seq(part):
    place = lax.axis_index("seq")
    for mask in SEQ_MASKS:
        rows = part.shape[0] // 2
        low = (place & mask) == 0
        keep = jnp.where(low, part[:rows], part[rows:])
        send = jnp.where(low, part[rows:], part[:rows]).astype(BF)
        part = keep + swap(send, "seq", mask).astype(F32)
    return part


def gather_blocks(own):
    beside = swap(own, "fsdp", 4)
    pair = jnp.stack([own, beside])
    left = shift_y(pair, 1)
    right = shift_y(pair, -1)
    far_own = shift_y(left[0], 1)
    far_beside = shift_y(right[1], -1)
    return (own, beside, left, right, far_own, far_beside)


def scatter_blocks(here, right, far, left):
    from_left = shift_y(far[0], 1)
    from_right = shift_y(far[1], -1)
    to_right = jnp.stack([(right[0].astype(F32) + from_left.astype(F32)).astype(BF), right[1]])
    to_left = jnp.stack([left[0], (left[1].astype(F32) + from_right.astype(F32)).astype(BF)])
    got_left = shift_y(to_right, 1)
    got_right = shift_y(to_left, -1)
    here = here + got_left.astype(F32) + got_right.astype(F32)
    return here[0] + swap(here[1].astype(BF), "fsdp", 4).astype(F32)


def over_seq(array):
    return lax.all_to_all(array, "seq", split_axis=0, concat_axis=0, tiled=True)


def joined(own, other, first):
    return jnp.where(
        first,
        jnp.concatenate([own, other], axis=1),
        jnp.concatenate([other, own], axis=1),
    )


def local(query_act, key_act, value_act, out_weight, reward_dir, guide_index, step_index):
    cfg = lax.axis_index("cfg")
    first = cfg == 0
    fsdp = lax.axis_index("fsdp")
    place = jnp.stack(
        [((fsdp // 4) ^ (r // 4)) * 4 + (fsdp + r) % 4 for r in range(8)] + [cfg]
    ).astype(jnp.int32)
    moment = step_index[0].astype(F32)
    gate = jnp.cos(0.5 * jnp.pi * (moment + 0.5) / STEPS)
    strength = 1.0 + GUIDE_STEP * guide_index[0].astype(F32)
    scalars = jnp.stack([gate, strength])

    half = out_weight.shape[1] // 2
    qkv = over_seq(pack_heads(query_act[0, 0], key_act[0, 0], value_act[0, 0]))
    own_half = jnp.where(first, out_weight[:, :half], out_weight[:, half:])
    blocks = gather_blocks(gather_seq(own_half))
    mixed_h, probs = attend_forward(qkv)
    mixed = over_seq(mixed_h)
    mixed_other = swap(mixed, "cfg", 1)
    guided, grad_out, keep, send = project(
        place, scalars, mixed, mixed_other, reward_dir[0], blocks
    )
    grad_mixed = (keep + swap(send, "cfg", 1).astype(F32)).astype(BF)
    grad_h = over_seq(grad_mixed)
    parts = weight_gradient(place, mixed, mixed_other, grad_out)
    grad_half = scatter_seq(scatter_blocks(*parts))
    grad_weight = joined(grad_half, swap(grad_half, "cfg", 1), first)
    guided_all = joined(guided, swap(guided, "cfg", 1), first)
    packed = over_seq(attend_backward(qkv, mixed_h, grad_h, probs))
    grad_query, grad_key, grad_value = unpack_heads(packed)
    return (
        guided_all[None],
        grad_query[None, None],
        grad_key[None, None],
        grad_value[None, None],
        grad_weight,
    )


def solution(mesh):
    placed = (
        P("cfg", "fsdp", "seq", None),
        P("cfg", "fsdp", "seq", None),
        P("cfg", "fsdp", "seq", None),
        P(("fsdp", "seq"), None),
        P("fsdp", "seq", None),
        P(),
        P(),
    )
    return jax.shard_map(
        local,
        mesh=mesh,
        in_specs=placed,
        out_specs=(
            P("fsdp", "seq", None),
            P("cfg", "fsdp", "seq", None),
            P("cfg", "fsdp", "seq", None),
            P("cfg", "fsdp", "seq", None),
            P(("fsdp", "seq"), None),
        ),
        check_vma=False,
    )
```

time: 1440 us -> 258 us (0.18)
  waiting for transfers between devices: 964 us -> 97.8 us
  blocking collectives: 101 us -> 0 us
  other arithmetic: 105 us -> 8.46 us
  local copies, waits for them, and re-layouts: 59.1 us -> 9.34 us
  matrix products: 46.8 us -> 0 us
  starting transfers between devices: 140 us -> 95.1 us
  Pallas kernels: 0 us -> 44.3 us
    reduce_scatter x1 -> x0, waiting for transfers between devices: 458 us -> none  [local(): lax.psum_scatter(lax.dot_general(columns, grad_out, (((0,), (0,)), ((), (...]
    all_gather x1 -> x0, waiting for transfers between devices: 441 us -> none  [local(): lax.all_gather(out_weight, ('fsdp', 'seq'), axis=0, tiled=True)]
    psum x1 -> x0, blocking collectives: 101 us -> none  [local(): lax.psum(partial_grad.astype(jnp.bfloat16), 'cfg').astype(jnp.float32)]
    unnamed x10 -> x0, other arithmetic: 94.7 us -> none
    ppermute x1 -> x22, waiting for transfers between devices: 0.69 us -> 91.1 us  [the longest x14 82.2 us: swap(): return lax.ppermute(value, axis, pairs)]
    all_to_all x8 -> x4, waiting for transfers between devices: 63.4 us -> 6.69 us  [over_seq(): return lax.all_to_all(array, 'seq', split_axis=0, concat_axis=0, tiled=True)]
    dot_general x31 -> x0, matrix products: 46.8 us -> none  [the longest x4 7.75 us: step(): jnp.einsum('bsqhd,bskhd->bshqk', query_part, keys_all, preferred_element_...]
    pallas_call x0 -> x6, Pallas kernels: none -> 44.3 us  [the longest x1 15.5 us: attend_forward(): pl.pallas_call(forward_kernel, grid=(shards // take,), out_shape=(jax.Sha...]
  transfers between devices with their start and end apart: 11 -> 26, of which waited for: 10 -> 12; matrix products, arithmetic and copies ran while one was open for 14% -> 4% of each run, Pallas kernels for 0% -> 11%
where the time goes in v1:
time: 258 us; the launch traced here: 257 us
  waiting for transfers between devices  97.8 us (38%)
  starting transfers between devices  95.1 us (37%)
  Pallas kernels  44.3 us (17%)
  local copies, waits for them, and re-layouts  9.34 us (4%)
  other arithmetic  8.46 us (3%)
    ppermute x14, waiting for transfers between devices, swap(): return lax.ppermute(value, axis, pairs)  82.2 us
    ppermute x14, starting transfers between devices, swap(): return lax.ppermute(value, axis, pairs)  56.4 us
    all_to_all x4, starting transfers between devices, over_seq(): return lax.all_to_all(array, 'seq', split_axis=0, concat_axis=0, tiled=True)  30.2 us
    pallas_call x1, Pallas kernels, attend_forward(): pl.pallas_call(forward_kernel, grid=(shards // take,), out_shape=(jax.Sha...  15.5 us
    pallas_call x1, Pallas kernels, attend_backward(): pl.pallas_call(backward_kernel, grid=(shards // take,), out_shape=jax.Sha...  13.3 us
    ppermute x8, waiting for transfers between devices, shift_y(): return lax.ppermute(value, 'fsdp', pairs)  8.89 us
    ppermute x8, starting transfers between devices, shift_y(): return lax.ppermute(value, 'fsdp', pairs)  8.56 us
    all_to_all x4, waiting for transfers between devices, over_seq(): return lax.all_to_all(array, 'seq', split_axis=0, concat_axis=0, tiled=True)  6.69 us
  transfers between devices with their start and end apart: 26, of which 12 were waited for; matrix products, arithmetic and copies ran while one was open for 4% of the time, Pallas kernels for 11%

profile of v1, /device:TPU:1, one launch (start us, length us, event | category | flops | bytes accessed | tf_op | source)
XLA Modules:
  0.0 257.3 jit_solution(16830205735275372253)
XLA Ops:
  3.4 10.2 %all-to-all-start = ((bf16[16,384,128]{2,1,0:T(8,128)(2,1)}), bf16[16,384,128]{2,1,0:T(8,128)(2,1)S(1)}, u32[]{:S(2)}, u32[]{:S(2)}) async-start(bf16[16,384,128]{2,1,0:T(8,128)(2,1)} %pack_heads.1), calls=%async_computation | async-start | bytes 3145728 | tf_op jit(solution)/shard_map/all_to_all | solution.py:323
  15.1 34.3 %collective-permute-done.1 = bf16[16,768]{1,0:T(8,128)(2,1)S(1)} collective-permute-done((bf16[16,768]{1,0:T(8,128)(2,1)S(1)}, bf16[16,768]{1,0:T(8,128)(2,1)S(1)}, u32[]{:S(2)}, u32[]{:S(2)}) %collective-permute-start.1) | collective-permute-done | bytes 24608 | tf_op jit(solution)/shard_map/ppermute | solution.py:275
  53.4 5.2 %collective-permute-start.3 = (bf16[64,768]{1,0:T(8,128)(2,1)S(1)}, bf16[64,768]{1,0:T(8,128)(2,1)S(1)}, u32[]{:S(2)}, u32[]{:S(2)}) collective-permute-start(bf16[64,768]{1,0:T(8,128)(2,1)S(1)} %maximum_select_fusion.4), channel_id=1, source_target_pairs={{0,4},{1,5},{2,6},{3,7},{4,0},{5,1},{6,2},{7,3},{8,12},{9,13},{10,... | collective-permute-start | bytes 294920 | tf_op jit(solution)/shard_map/ppermute | solution.py:275
  62.3 3.3 %collective-permute-done.4 = bf16[128,768]{1,0:T(8,128)(2,1)S(1)} collective-permute-done((bf16[128,768]{1,0:T(8,128)(2,1)S(1)}, bf16[128,768]{1,0:T(8,128)(2,1)S(1)}, u32[]{:S(2)}, u32[]{:S(2)}) %collective-permute-start.4) | collective-permute-done | bytes 196640 | tf_op jit(solution)/shard_map/ppermute | solution.py:275
  68.3 7.7 %collective-permute-done.5.w1 = bf16[256,768]{1,0:T(8,128)(2,1)S(1)} collective-permute-done((bf16[256,768]{1,0:T(8,128)(2,1)S(1)}, bf16[256,768]{1,0:T(8,128)(2,1)S(1)}, u32[]{:S(2)}, u32[]{:S(2)}) %collective-permute-start.5) | collective-permute-done | bytes 393248 | tf_op jit(solution)/shard_map/ppermute | solution.py:275
  81.6 15.5 %attend_forward.1 = (bf16[16,128,128]{2,1,0:T(8,128)(2,1)}, bf16[2048,2048]{1,0:T(8,128)(2,1)}) custom-call(bf16[16,384,128]{2,1,0:T(8,128)(2,1)} %copy-done), custom_call_target="tpu_custom_call" | custom-call | tf_op jit(solution)/shard_map/attend_forward/pallas_call | solution.py:99
  97.1 7.2 %all-to-all-start.1 = ((bf16[16,128,128]{2,1,0:T(8,128)(2,1)}), bf16[16,128,128]{2,1,0:T(8,128)(2,1)S(1)}, u32[]{:S(2)}, u32[]{:S(2)}) async-start(bf16[16,128,128]{2,1,0:T(8,128)(2,1)} %get-tuple-element.18.mixed_ref), calls=%async_computation.1 | async-start | bytes 1048576 | tf_op jit(solution)/shard_map/all_to_all | solution.py:323
  107.9 6.7 %all-to-all-done.1.own_ref = bf16[16,128,128]{2,1,0:T(8,128)(2,1)S(1)} async-done(((bf16[16,128,128]{2,1,0:T(8,128)(2,1)}), bf16[16,128,128]{2,1,0:T(8,128)(2,1)S(1)}, u32[]{:S(2)}, u32[]{:S(2)}) %all-to-all-start.1) | async-done | bytes 524320 | tf_op jit(solution)/shard_map/all_to_all | solution.py:323
  114.6 7.3 %collective-permute-start = (bf16[16,128,128]{2,1,0:T(8,128)(2,1)S(1)}, bf16[16,128,128]{2,1,0:T(8,128)(2,1)S(1)}, u32[]{:S(2)}, u32[]{:S(2)}) collective-permute-start(bf16[16,128,128]{2,1,0:T(8,128)(2,1)S(1)} %all-to-all-done.1.own_ref), channel_id=1, source_target_pairs={{0,128},{128,0},{1,129},{129,1},{2,130},{130,2},{3,131},{131,3},{4... | collective-permute-start | bytes 1572872 | tf_op jit(solution)/shard_map/ppermute | solution.py:275
  125.3 5.5 %collective-permute-done.8.w4 = bf16[256,768]{1,0:T(8,128)(2,1)S(1)} collective-permute-done((bf16[256,768]{1,0:T(8,128)(2,1)}, bf16[256,768]{1,0:T(8,128)(2,1)S(1)}, u32[]{:S(2)}, u32[]{:S(2)}) %collective-permute-start.8) | collective-permute-done | bytes 393248 | tf_op jit(solution)/shard_map/ppermute | solution.py:270
  131.7 5.7 %project.1 = (bf16[128,768]{1,0:T(8,128)(2,1)}, bf16[256,768]{1,0:T(8,128)(2,1)}, f32[16,128,128]{2,1,0:T(8,128)}, bf16[16,128,128]{2,1,0:T(8,128)(2,1)}) custom-call(s32[9]{0:T(128)} %stack.63.place_ref, f32[2]{0:T(128)} %pad_maximum_fusion.3.scalar_ref, bf16[16,128,128]{2,1,0:T(8,128)(2,1)} %copy-done.2, bf16[16,128,128]{2,1,0:T(8,128)(2,1)} %copy-done.3, ...), custom_call_target="tpu_custom_call" | custom-call | tf_op jit(solution)/shard_map/project/pallas_call | solution.py:226
  137.5 4.0 %weight_gradient.1 = (f32[2,256,768]{2,1,0:T(8,128)}, bf16[2,256,768]{2,1,0:T(8,128)(2,1)}, bf16[2,256,768]{2,1,0:T(8,128)(2,1)}, bf16[2,256,768]{2,1,0:T(8,128)(2,1)}) custom-call(s32[9]{0:T(128)} %stack.63.place_ref, bf16[16,128,128]{2,1,0:T(8,128)(2,1)} %copy-done.2, bf16[16,128,128]{2,1,0:T(8,128)(2,1)} %copy-done.3, ...), custom_call_target="tpu_custom_call" | custom-call | tf_op jit(solution)/shard_map/weight_gradient/pallas_call | solution.py:253
  144.3 5.5 %collective-permute-start.11 = (bf16[16,128,128]{2,1,0:T(8,128)(2,1)S(1)}, bf16[16,128,128]{2,1,0:T(8,128)(2,1)S(1)}, u32[]{:S(2)}, u32[]{:S(2)}) collective-permute-start(bf16[16,128,128]{2,1,0:T(8,128)(2,1)S(1)} %copy-done.17), channel_id=1, source_target_pairs={{0,128},{128,0},{1,129},{129,1},{2,130},{130,2},{3,131},{131,3},{4... | collective-permute-start | bytes 1572872 | tf_op jit(solution)/shard_map/ppermute | solution.py:275
  153.7 9.1 %all-to-all-start.2 = ((bf16[16,128,128]{2,1,0:T(8,128)(2,1)}), bf16[16,128,128]{2,1,0:T(8,128)(2,1)S(1)}, u32[]{:S(2)}, u32[]{:S(2)}) async-start(bf16[16,128,128]{2,1,0:T(8,128)(2,1)} %add_convert_fusion), calls=%async_computation.2 | async-start | bytes 1048576 | tf_op jit(solution)/shard_map/all_to_all | solution.py:323
  169.0 10.3 %collective-permute-start.16 = (bf16[256,768]{1,0:T(8,128)(2,1)S(1)}, bf16[256,768]{1,0:T(8,128)(2,1)}, u32[]{:S(2)}, u32[]{:S(2)}) collective-permute-start(bf16[256,768]{1,0:T(8,128)(2,1)S(1)} %fusion.5), channel_id=1, source_target_pairs={{0,64},{16,80},{32,96},{48,112},{64,0},{80,16},{96,32},{112,48},{1... | collective-permute-start | bytes 1179656 | tf_op jit(solution)/shard_map/ppermute | solution.py:275
  180.0 13.3 %attend_backward.1 = bf16[16,384,128]{2,1,0:T(8,128)(2,1)} custom-call(bf16[16,384,128]{2,1,0:T(8,128)(2,1)} %copy-done, bf16[16,128,128]{2,1,0:T(8,128)(2,1)} %get-tuple-element.18.mixed_ref, bf16[16,128,128]{2,1,0:T(8,128)(2,1)} %copy-done.4, bf16[2048,2048]{1,0:T(8,128)(2,1)} %get-tuple-element.22.probs_ref), custom_call_target="tpu_custom_call" | custom-call | tf_op jit(solution)/shard_map/attend_backward/pallas_call | solution.py:159
  193.3 3.7 %all-to-all-start.3 = ((bf16[16,384,128]{2,1,0:T(8,128)(2,1)}), bf16[16,384,128]{2,1,0:T(8,128)(2,1)S(1)}, u32[]{:S(2)}, u32[]{:S(2)}) async-start(bf16[16,384,128]{2,1,0:T(8,128)(2,1)} %attend_backward.1), calls=%async_computation.3 | async-start | bytes 3145728 | tf_op jit(solution)/shard_map/all_to_all | solution.py:323
  199.5 5.8 %collective-permute-done.17 = bf16[128,768]{1,0:T(8,128)(2,1)S(1)} collective-permute-done((bf16[128,768]{1,0:T(8,128)(2,1)S(1)}, bf16[128,768]{1,0:T(8,128)(2,1)S(1)}, u32[]{:S(2)}, u32[]{:S(2)}) %collective-permute-start.17) | collective-permute-done | bytes 196640 | tf_op jit(solution)/shard_map/ppermute | solution.py:275
  205.4 7.1 %collective-permute-start.18 = (bf16[64,768]{1,0:T(8,128)(2,1)S(1)}, bf16[64,768]{1,0:T(8,128)(2,1)S(1)}, u32[]{:S(2)}, u32[]{:S(2)}) collective-permute-start(bf16[64,768]{1,0:T(8,128)(2,1)S(1)} %select_convert_fusion.1), channel_id=1, source_target_pairs={{0,4},{1,5},{2,6},{3,7},{4,0},{5,1},{6,2},{7,3},{8,12},{9,13},{10,... | collective-permute-start | bytes 294920 | tf_op jit(solution)/shard_map/ppermute | solution.py:275
  212.5 21.3 %collective-permute-done.18 = bf16[64,768]{1,0:T(8,128)(2,1)S(1)} collective-permute-done((bf16[64,768]{1,0:T(8,128)(2,1)S(1)}, bf16[64,768]{1,0:T(8,128)(2,1)S(1)}, u32[]{:S(2)}, u32[]{:S(2)}) %collective-permute-start.18) | collective-permute-done | bytes 98336 | tf_op jit(solution)/shard_map/ppermute | solution.py:275
  234.2 4.7 %collective-permute-done.19 = bf16[32,768]{1,0:T(8,128)(2,1)S(1)} collective-permute-done((bf16[32,768]{1,0:T(8,128)(2,1)S(1)}, bf16[32,768]{1,0:T(8,128)(2,1)S(1)}, u32[]{:S(2)}, u32[]{:S(2)}) %collective-permute-start.19) | collective-permute-done | bytes 49184 | tf_op jit(solution)/shard_map/ppermute | solution.py:275
  238.9 3.6 %collective-permute-start.20 = (bf16[16,768]{1,0:T(8,128)(2,1)S(1)}, bf16[16,768]{1,0:T(8,128)(2,1)S(1)}, u32[]{:S(2)}, u32[]{:S(2)}) collective-permute-start(bf16[16,768]{1,0:T(8,128)(2,1)S(1)} %select_convert_fusion.3), channel_id=1, source_target_pairs={{0,1},{1,0},{2,3},{3,2},{4,5},{5,4},{6,7},{7,6},{8,9},{9,8},{10,11... | collective-permute-start | bytes 73736 | tf_op jit(solution)/shard_map/ppermute | solution.py:275
  242.5 5.4 %collective-permute-start.10 = (bf16[128,768]{1,0:T(8,128)(2,1)S(1)}, bf16[128,768]{1,0:T(8,128)(2,1)S(1)}, u32[]{:S(2)}, u32[]{:S(2)}) collective-permute-start(bf16[128,768]{1,0:T(8,128)(2,1)S(1)} %copy-done.15), channel_id=1, source_target_pairs={{0,128},{128,0},{1,129},{129,1},{2,130},{130,2},{3,131},{131,3},{4... | collective-permute-start | bytes 589832 | tf_op jit(solution)/shard_map/ppermute | solution.py:275
  247.9 3.8 %collective-permute-start.21 = (f32[16,768]{1,0:T(8,128)S(1)}, f32[16,768]{1,0:T(8,128)S(1)}, u32[]{:S(2)}, u32[]{:S(2)}) collective-permute-start(f32[16,768]{1,0:T(8,128)S(1)} %convert_add_fusion.6), channel_id=1, source_target_pairs={{0,128},{128,0},{1,129},{129,1},{2,130},{130,2},{3,131},{131,3},{4... | collective-permute-start | bytes 147464 | tf_op jit(solution)/shard_map/ppermute | solution.py:275
  (102 shorter events, 48.9 us)
Async XLA Ops:
  3.4 77.0 %all-to-all-start = ((bf16[16,384,128]{2,1,0:T(8,128)(2,1)}), bf16[16,384,128]{2,1,0:T(8,128)(2,1)S(1)}, u32[]{:S(2)}, u32[]{:S(2)}) async-start(bf16[16,384,128]{2,1,0:T(8,128)(2,1)} %pack_heads.1), calls=%async_computation | async-start | bytes 3145728 | tf_op jit(solution)/shard_map/all_to_all | solution.py:323
  13.7 35.7 %collective-permute-start.1 = (bf16[16,768]{1,0:T(8,128)(2,1)S(1)}, bf16[16,768]{1,0:T(8,128)(2,1)S(1)}, u32[]{:S(2)}, u32[]{:S(2)}) collective-permute-start(bf16[16,768]{1,0:T(8,128)(2,1)S(1)} %slice_select_fusion), channel_id=1, source_target_pairs={{0,1},{1,0},{2,3},{3,2},{4,5},{5,4},{6,7},{7,6},{8,9},{9,8},{10,11... | collective-permute-start | bytes 73736 | tf_op jit(solution)/shard_map/ppermute | solution.py:275
  53.4 7.5 %collective-permute-start.3 = (bf16[64,768]{1,0:T(8,128)(2,1)S(1)}, bf16[64,768]{1,0:T(8,128)(2,1)S(1)}, u32[]{:S(2)}, u32[]{:S(2)}) collective-permute-start(bf16[64,768]{1,0:T(8,128)(2,1)S(1)} %maximum_select_fusion.4), channel_id=1, source_target_pairs={{0,4},{1,5},{2,6},{3,7},{4,0},{5,1},{6,2},{7,3},{8,12},{9,13},{10,... | collective-permute-start | bytes 294920 | tf_op jit(solution)/shard_map/ppermute | solution.py:275
  65.6 10.3 %collective-permute-start.5 = (bf16[256,768]{1,0:T(8,128)(2,1)S(1)}, bf16[256,768]{1,0:T(8,128)(2,1)S(1)}, u32[]{:S(2)}, u32[]{:S(2)}) collective-permute-start(bf16[256,768]{1,0:T(8,128)(2,1)S(1)} %maximum_select_fusion.w0), channel_id=1, source_target_pairs={{0,64},{16,80},{32,96},{48,112},{64,0},{80,16},{96,32},{112,48},{1... | collective-permute-start | bytes 1179656 | tf_op jit(solution)/shard_map/ppermute | solution.py:275
  77.7 26.7 %collective-permute-start.7 = (bf16[2,256,768]{2,1,0:T(8,128)(2,1)}, bf16[2,256,768]{2,1,0:T(8,128)(2,1)S(1)}, u32[]{:S(2)}, u32[]{:S(2)}) collective-permute-start(bf16[2,256,768]{2,1,0:T(8,128)(2,1)} %pad_maximum_fusion), channel_id=1, source_target_pairs={{0,48},{16,0},{32,16},{48,32},{64,112},{80,64},{96,80},{112,96},{1... | collective-permute-start | bytes 2359304 | tf_op jit(solution)/shard_map/ppermute | solution.py:270
  97.1 17.5 %all-to-all-start.1 = ((bf16[16,128,128]{2,1,0:T(8,128)(2,1)}), bf16[16,128,128]{2,1,0:T(8,128)(2,1)S(1)}, u32[]{:S(2)}, u32[]{:S(2)}) async-start(bf16[16,128,128]{2,1,0:T(8,128)(2,1)} %get-tuple-element.18.mixed_ref), calls=%async_computation.1 | async-start | bytes 1048576 | tf_op jit(solution)/shard_map/all_to_all | solution.py:323
  104.3 17.6 %collective-permute-start.6 = (bf16[2,256,768]{2,1,0:T(8,128)(2,1)}, bf16[2,256,768]{2,1,0:T(8,128)(2,1)S(1)}, u32[]{:S(2)}, u32[]{:S(2)}) collective-permute-start(bf16[2,256,768]{2,1,0:T(8,128)(2,1)} %pad_maximum_fusion), channel_id=1, source_target_pairs={{0,16},{16,32},{32,48},{48,0},{64,80},{80,96},{96,112},{112,64},{1... | collective-permute-start | bytes 2359304 | tf_op jit(solution)/shard_map/ppermute | solution.py:270
  105.3 20.0 %collective-permute-start.9 = (bf16[256,768]{1,0:T(8,128)(2,1)}, bf16[256,768]{1,0:T(8,128)(2,1)S(1)}, u32[]{:S(2)}, u32[]{:S(2)}) collective-permute-start(bf16[256,768]{1,0:T(8,128)(2,1)} %slice_bitcast_fusion.1), channel_id=1, source_target_pairs={{0,48},{16,0},{32,16},{48,32},{64,112},{80,64},{96,80},{112,96},{1... | collective-permute-start | bytes 1179656 | tf_op jit(solution)/shard_map/ppermute | solution.py:270
  114.6 16.2 %collective-permute-start = (bf16[16,128,128]{2,1,0:T(8,128)(2,1)S(1)}, bf16[16,128,128]{2,1,0:T(8,128)(2,1)S(1)}, u32[]{:S(2)}, u32[]{:S(2)}) collective-permute-start(bf16[16,128,128]{2,1,0:T(8,128)(2,1)S(1)} %all-to-all-done.1.own_ref), channel_id=1, source_target_pairs={{0,128},{128,0},{1,129},{129,1},{2,130},{130,2},{3,131},{131,3},{4... | collective-permute-start | bytes 1572872 | tf_op jit(solution)/shard_map/ppermute | solution.py:275
  122.8 8.0 %collective-permute-start.8 = (bf16[256,768]{1,0:T(8,128)(2,1)}, bf16[256,768]{1,0:T(8,128)(2,1)S(1)}, u32[]{:S(2)}, u32[]{:S(2)}) collective-permute-start(bf16[256,768]{1,0:T(8,128)(2,1)} %slice_bitcast_fusion.2), channel_id=1, source_target_pairs={{0,16},{16,32},{32,48},{48,0},{64,80},{80,96},{96,112},{112,64},{1... | collective-permute-start | bytes 1179656 | tf_op jit(solution)/shard_map/ppermute | solution.py:270
  142.8 7.2 %collective-permute-start.14 = (bf16[256,768]{1,0:T(8,128)(2,1)S(1)}, bf16[256,768]{1,0:T(8,128)(2,1)S(1)}, u32[]{:S(2)}, u32[]{:S(2)}) collective-permute-start(bf16[256,768]{1,0:T(8,128)(2,1)S(1)} %get-tuple-element.32), channel_id=1, source_target_pairs={{0,48},{16,0},{32,16},{48,32},{64,112},{80,64},{96,80},{112,96},{1... | collective-permute-start | bytes 1179656 | tf_op jit(solution)/shard_map/ppermute | solution.py:270
  143.3 8.1 %collective-permute-start.12 = (bf16[256,768]{1,0:T(8,128)(2,1)S(1)}, bf16[256,768]{1,0:T(8,128)(2,1)S(1)}, u32[]{:S(2)}, u32[]{:S(2)}) collective-permute-start(bf16[256,768]{1,0:T(8,128)(2,1)S(1)} %get-tuple-element.31), channel_id=1, source_target_pairs={{0,16},{16,32},{32,48},{48,0},{64,80},{80,96},{96,112},{112,64},{1... | collective-permute-start | bytes 1179656 | tf_op jit(solution)/shard_map/ppermute | solution.py:270
  144.3 8.4 %collective-permute-start.11 = (bf16[16,128,128]{2,1,0:T(8,128)(2,1)S(1)}, bf16[16,128,128]{2,1,0:T(8,128)(2,1)S(1)}, u32[]{:S(2)}, u32[]{:S(2)}) collective-permute-start(bf16[16,128,128]{2,1,0:T(8,128)(2,1)S(1)} %copy-done.17), channel_id=1, source_target_pairs={{0,128},{128,0},{1,129},{129,1},{2,130},{130,2},{3,131},{131,3},{4... | collective-permute-start | bytes 1572872 | tf_op jit(solution)/shard_map/ppermute | solution.py:275
  150.1 15.8 %collective-permute-start.15 = (bf16[2,256,768]{2,1,0:T(8,128)(2,1)S(1)}, bf16[2,256,768]{2,1,0:T(8,128)(2,1)S(1)}, u32[]{:S(2)}, u32[]{:S(2)}) collective-permute-start(bf16[2,256,768]{2,1,0:T(8,128)(2,1)S(1)} %pad_maximum_fusion.2), channel_id=1, source_target_pairs={{0,48},{16,0},{32,16},{48,32},{64,112},{80,64},{96,80},{112,96},{1... | collective-permute-start | bytes 2359304 | tf_op jit(solution)/shard_map/ppermute | solution.py:270
  152.5 13.7 %collective-permute-start.13 = (bf16[2,256,768]{2,1,0:T(8,128)(2,1)}, bf16[2,256,768]{2,1,0:T(8,128)(2,1)S(1)}, u32[]{:S(2)}, u32[]{:S(2)}) collective-permute-start(bf16[2,256,768]{2,1,0:T(8,128)(2,1)} %pad_maximum_fusion.1), channel_id=1, source_target_pairs={{0,16},{16,32},{32,48},{48,0},{64,80},{80,96},{96,112},{112,64},{1... | collective-permute-start | bytes 2359304 | tf_op jit(solution)/shard_map/ppermute | solution.py:270
  153.7 25.5 %all-to-all-start.2 = ((bf16[16,128,128]{2,1,0:T(8,128)(2,1)}), bf16[16,128,128]{2,1,0:T(8,128)(2,1)S(1)}, u32[]{:S(2)}, u32[]{:S(2)}) async-start(bf16[16,128,128]{2,1,0:T(8,128)(2,1)} %add_convert_fusion), calls=%async_computation.2 | async-start | bytes 1048576 | tf_op jit(solution)/shard_map/all_to_all | solution.py:323
  169.0 28.1 %collective-permute-start.16 = (bf16[256,768]{1,0:T(8,128)(2,1)S(1)}, bf16[256,768]{1,0:T(8,128)(2,1)}, u32[]{:S(2)}, u32[]{:S(2)}) collective-permute-start(bf16[256,768]{1,0:T(8,128)(2,1)S(1)} %fusion.5), channel_id=1, source_target_pairs={{0,64},{16,80},{32,96},{48,112},{64,0},{80,16},{96,32},{112,48},{1... | collective-permute-start | bytes 1179656 | tf_op jit(solution)/shard_map/ppermute | solution.py:275
  193.3 59.9 %all-to-all-start.3 = ((bf16[16,384,128]{2,1,0:T(8,128)(2,1)}), bf16[16,384,128]{2,1,0:T(8,128)(2,1)S(1)}, u32[]{:S(2)}, u32[]{:S(2)}) async-start(bf16[16,384,128]{2,1,0:T(8,128)(2,1)} %attend_backward.1), calls=%async_computation.3 | async-start | bytes 3145728 | tf_op jit(solution)/shard_map/all_to_all | solution.py:323
  198.1 7.2 %collective-permute-start.17 = (bf16[128,768]{1,0:T(8,128)(2,1)S(1)}, bf16[128,768]{1,0:T(8,128)(2,1)S(1)}, u32[]{:S(2)}, u32[]{:S(2)}) collective-permute-start(bf16[128,768]{1,0:T(8,128)(2,1)S(1)} %select_convert_fusion), channel_id=1, source_target_pairs={{0,8},{1,9},{2,10},{3,11},{4,12},{5,13},{6,14},{7,15},{8,0},{9,1},... | collective-permute-start | bytes 589832 | tf_op jit(solution)/shard_map/ppermute | solution.py:275
  205.4 28.3 %collective-permute-start.18 = (bf16[64,768]{1,0:T(8,128)(2,1)S(1)}, bf16[64,768]{1,0:T(8,128)(2,1)S(1)}, u32[]{:S(2)}, u32[]{:S(2)}) collective-permute-start(bf16[64,768]{1,0:T(8,128)(2,1)S(1)} %select_convert_fusion.1), channel_id=1, source_target_pairs={{0,4},{1,5},{2,6},{3,7},{4,0},{5,1},{6,2},{7,3},{8,12},{9,13},{10,... | collective-permute-start | bytes 294920 | tf_op jit(solution)/shard_map/ppermute | solution.py:275
  233.8 5.0 %collective-permute-start.19 = (bf16[32,768]{1,0:T(8,128)(2,1)S(1)}, bf16[32,768]{1,0:T(8,128)(2,1)S(1)}, u32[]{:S(2)}, u32[]{:S(2)}) collective-permute-start(bf16[32,768]{1,0:T(8,128)(2,1)S(1)} %select_convert_fusion.2), channel_id=1, source_target_pairs={{0,2},{1,3},{2,0},{3,1},{4,6},{5,7},{6,4},{7,5},{8,10},{9,11},{10,... | collective-permute-start | bytes 147464 | tf_op jit(solution)/shard_map/ppermute | solution.py:275
  238.9 9.0 %collective-permute-start.20 = (bf16[16,768]{1,0:T(8,128)(2,1)S(1)}, bf16[16,768]{1,0:T(8,128)(2,1)S(1)}, u32[]{:S(2)}, u32[]{:S(2)}) collective-permute-start(bf16[16,768]{1,0:T(8,128)(2,1)S(1)} %select_convert_fusion.3), channel_id=1, source_target_pairs={{0,1},{1,0},{2,3},{3,2},{4,5},{5,4},{6,7},{7,6},{8,9},{9,8},{10,11... | collective-permute-start | bytes 73736 | tf_op jit(solution)/shard_map/ppermute | solution.py:275
  242.5 9.2 %collective-permute-start.10 = (bf16[128,768]{1,0:T(8,128)(2,1)S(1)}, bf16[128,768]{1,0:T(8,128)(2,1)S(1)}, u32[]{:S(2)}, u32[]{:S(2)}) collective-permute-start(bf16[128,768]{1,0:T(8,128)(2,1)S(1)} %copy-done.15), channel_id=1, source_target_pairs={{0,128},{128,0},{1,129},{129,1},{2,130},{130,2},{3,131},{131,3},{4... | collective-permute-start | bytes 589832 | tf_op jit(solution)/shard_map/ppermute | solution.py:275
  247.9 4.7 %collective-permute-start.21 = (f32[16,768]{1,0:T(8,128)S(1)}, f32[16,768]{1,0:T(8,128)S(1)}, u32[]{:S(2)}, u32[]{:S(2)}) collective-permute-start(f32[16,768]{1,0:T(8,128)S(1)} %convert_add_fusion.6), channel_id=1, source_target_pairs={{0,128},{128,0},{1,129},{129,1},{2,130},{130,2},{3,131},{131,3},{4... | collective-permute-start | bytes 147464 | tf_op jit(solution)/shard_map/ppermute | solution.py:275
  (20 other events, 184.4 us)

commit v2 on v1

v2 whole, which is shorter than its diff:
```python
import functools

import jax
import jax.numpy as jnp
from jax import lax
from jax.experimental import pallas as pl
from jax.experimental.pallas import tpu as pltpu
from jax.sharding import PartitionSpec as P

HDIM = 128
STEPS = 50
GUIDE_STEP = 0.04
LOG2E = 1.4426950408889634
BF = jnp.bfloat16
F32 = jnp.float32
NT = (((1,), (1,)), ((), ()))
VMEM_LIMIT = 56 * 1024 * 1024
EXTRA = 48


def params():
    return pltpu.CompilerParams(vmem_limit_bytes=VMEM_LIMIT)


def whole(count):
    return [pl.BlockSpec(memory_space=pltpu.VMEM) for _ in range(count)]


def anywhere():
    return pl.BlockSpec(memory_space=pl.ANY)


def scalars_spec():
    return pl.BlockSpec(memory_space=pltpu.SMEM)


def call(kernel, name, out_shape, in_specs, out_specs=None, **kwargs):
    if out_specs is None:
        out_specs = whole(len(out_shape)) if isinstance(out_shape, tuple) else whole(1)[0]
    return pl.pallas_call(
        kernel,
        out_shape=out_shape,
        in_specs=in_specs,
        out_specs=tuple(out_specs) if isinstance(out_shape, tuple) else out_specs,
        compiler_params=params(),
        name=name,
        **kwargs,
    )


def shaped(shape, dtype=BF):
    return jax.ShapeDtypeStruct(shape, dtype)


def lanes_of(head):
    return slice(head * HDIM, (head + 1) * HDIM)


def pack_first_kernel(place_ref, q_ref, k_ref, w_ref, out_ref):
    rows = q_ref.shape[0]
    deep = w_ref.shape[0]
    first = place_ref[0] == 0
    half = w_ref.shape[1] // 2
    picked = jnp.where(first, w_ref[:, :half], w_ref[:, half:])
    heads = out_ref.shape[0]
    per = EXTRA // deep
    for head in range(heads):
        side = head // (heads // 2)
        for part in range(per):
            out_ref[head, part * deep : (part + 1) * deep, :] = picked[:, lanes_of(side * per + part)]
        out_ref[head, EXTRA : EXTRA + rows, :] = q_ref[:, lanes_of(head)]
        out_ref[head, EXTRA + rows :, :] = k_ref[:, lanes_of(head)]


def pack_first(place, query, key, weight):
    rows, width = query.shape
    return call(
        pack_first_kernel,
        "pack_first",
        shaped((width // HDIM, EXTRA + 2 * rows, HDIM)),
        [scalars_spec()] + whole(3),
    )(place, query, key, weight)


def pack_kernel(in_ref, out_ref):
    for head in range(out_ref.shape[0]):
        out_ref[head] = in_ref[:, lanes_of(head)]


def pack_heads(array):
    rows, width = array.shape
    return call(pack_kernel, "pack_heads", shaped((width // HDIM, rows, HDIM)), whole(1))(array)


def unpack_kernel(in_ref, *out_refs):
    rows = out_refs[0].shape[0]
    skip = in_ref.shape[1] - rows * len(out_refs)
    for head in range(in_ref.shape[0]):
        for place, ref in enumerate(out_refs):
            start = skip + place * rows
            ref[:, lanes_of(head)] = in_ref[head, start : start + rows, :]


def unpack_heads(packed, count, rows):
    out = shaped((rows, packed.shape[0] * HDIM))
    return call(unpack_kernel, "unpack_heads", (out,) * count, whole(1))(packed)


def extra_spec(packed):
    return pl.BlockSpec((packed.shape[0], EXTRA, HDIM), lambda i: (0, 0, 0))


def piece_kernel(in_ref, out_ref):
    per = out_ref.shape[1] // HDIM
    deep = EXTRA // per
    for source in range(in_ref.shape[0]):
        for part in range(per):
            out_ref[source * deep : (source + 1) * deep, lanes_of(part)] = in_ref[
                source, part * deep : (part + 1) * deep, :
            ]


def weight_piece(packed, deep):
    return call(
        piece_kernel,
        "weight_piece",
        shaped((packed.shape[0] * deep, EXTRA // deep * HDIM)),
        [extra_spec(packed)],
        grid=(1,),
    )(packed)


def probs_kernel(first_ref, order_ref, probs_ref):
    shards, total_rows, _ = first_ref.shape
    rows = (total_rows - EXTRA) // 2
    length = shards * rows
    step = pl.program_id(0)
    take = probs_ref.shape[1] // rows
    query = first_ref[pl.ds(step * take, take), EXTRA : EXTRA + rows, :].reshape(take * rows, HDIM)
    keys = first_ref[:, EXTRA + rows :, :].reshape(length, HDIM)
    scores = lax.dot_general(keys, query, NT, preferred_element_type=F32)
    scale = HDIM ** (-0.5) * LOG2E
    peak = jnp.max(scores, axis=0, keepdims=True) * scale
    weights = jnp.exp2(scores * scale - peak)
    total = jnp.sum(weights, axis=0, keepdims=True)
    probs_ref[...] = (weights * (1.0 / total)).astype(BF)


def probabilities(first, order):
    shards, total_rows, _ = first.shape
    rows = (total_rows - EXTRA) // 2
    length = shards * rows
    take = 2
    return call(
        probs_kernel,
        "probabilities",
        shaped((length, length)),
        whole(1) + [anywhere()],
        pl.BlockSpec((length, take * rows), lambda i: (0, i)),
        grid=(shards // take,),
    )(first, order)


def mix_kernel(value_ref, probs_ref, out_ref, value_t):
    shards, rows, _ = value_ref.shape

    @pl.when(pl.program_id(0) == 0)
    def _():
        value_t[...] = value_ref[...].reshape(shards * rows, HDIM).astype(F32).T.astype(BF)

    mixed_t = jnp.dot(value_t[...], probs_ref[...], preferred_element_type=F32)
    out_ref[...] = mixed_t.T.astype(BF).reshape(out_ref.shape)


def mix(value, probs):
    shards, rows, _ = value.shape
    length = shards * rows
    take = 2
    return call(
        mix_kernel,
        "mix",
        shaped(value.shape),
        whole(1) + [pl.BlockSpec((length, take * rows), lambda i: (0, i))],
        pl.BlockSpec((take, rows, HDIM), lambda i: (i, 0, 0)),
        grid=(shards // take,),
        scratch_shapes=[pltpu.VMEM((HDIM, length), BF)],
    )(value, probs)


def grad_value_kernel(grad_ref, probs_ref, out_ref):
    shards, rows, _ = grad_ref.shape
    grad = grad_ref[...].reshape(shards * rows, HDIM)
    part = jnp.dot(probs_ref[...], grad, preferred_element_type=F32)
    out_ref[...] = part.astype(BF).reshape(out_ref.shape)


def grad_of_value(grad, probs):
    shards, rows, _ = grad.shape
    length = shards * rows
    take = 2
    return call(
        grad_value_kernel,
        "grad_of_value",
        shaped(grad.shape),
        whole(1) + [pl.BlockSpec((take * rows, length), lambda i: (i, 0))],
        pl.BlockSpec((take, rows, HDIM), lambda i: (i, 0, 0)),
        grid=(shards // take,),
    )(grad, probs)


def backward_kernel(first_ref, value_ref, mixed_ref, grad_ref, order_ref, probs_ref, out_ref, inner, query_t):
    shards, rows, _ = value_ref.shape
    length = shards * rows
    step = pl.program_id(0)
    block = probs_ref.shape[0]
    take = block // rows
    factor = HDIM ** (-0.5)
    grad = grad_ref[...].reshape(length, HDIM)

    @pl.when(step == 0)
    def _():
        mixed = mixed_ref[...].reshape(length, HDIM)
        product = grad.astype(F32) * mixed.astype(F32)
        inner[...] = jnp.sum(product.T, axis=0, keepdims=True)
        query_t[...] = jnp.zeros_like(query_t)

    query = first_ref[:, EXTRA : EXTRA + rows, :].reshape(length, HDIM)
    here = pl.ds(step * take, take)
    keys = first_ref[here, EXTRA + rows :, :].reshape(block, HDIM)
    value = value_ref[here].reshape(block, HDIM)
    probs = probs_ref[...]
    grad_probs = lax.dot_general(value, grad, NT, preferred_element_type=F32)
    grad_scores = (probs.astype(F32) * (grad_probs - inner[...])).astype(BF)
    grad_key = jnp.dot(grad_scores, query, preferred_element_type=F32) * factor
    out_ref[here, EXTRA + rows :, :] = grad_key.astype(BF).reshape(take, rows, HDIM)
    keys_t = keys.astype(F32).T.astype(BF)
    query_t[...] += jnp.dot(keys_t, grad_scores, preferred_element_type=F32)

    @pl.when(step == pl.num_programs(0) - 1)
    def _():
        grad_query = (query_t[...] * factor).T.astype(BF)
        out_ref[:, EXTRA : EXTRA + rows, :] = grad_query.reshape(shards, rows, HDIM)
        out_ref[:, :EXTRA, :] = jnp.zeros((shards, EXTRA, HDIM), BF)


def attend_backward(first, value, mixed, grad, order, probs):
    shards, rows, _ = value.shape
    length = shards * rows
    take = 2
    return call(
        backward_kernel,
        "attend_backward",
        shaped(first.shape),
        whole(4) + [anywhere(), pl.BlockSpec((take * rows, length), lambda i: (i, 0))],
        whole(1)[0],
        grid=(shards // take,),
        scratch_shapes=[pltpu.VMEM((1, length), F32), pltpu.VMEM((HDIM, length), F32)],
    )(first, value, mixed, grad, order, probs)


def piece_place(place_ref, slot):
    block = place_ref[1 + 2 * slot]
    side = place_ref[2 + 2 * slot]
    return block, side


def assemble_kernel(place_ref, *refs):
    pairs, out_ref, sems = refs[:8], refs[8], refs[9]
    deep, wide = pairs[0].shape[1:]
    copies = []
    for slot in range(16):
        block, side = piece_place(place_ref, slot)
        rows = pl.ds(pl.multiple_of(block * deep, deep), deep)
        lanes = pl.ds(pl.multiple_of(side * wide, HDIM), wide)
        copies.append(
            pltpu.make_async_copy(
                pairs[slot // 2].at[slot % 2], out_ref.at[rows, lanes], sems.at[slot]
            )
        )
    for copy in copies:
        copy.start()
    for copy in copies:
        copy.wait()


def assemble(place, pairs):
    _, deep, wide = pairs[0].shape
    return call(
        assemble_kernel,
        "assemble",
        shaped((8 * deep, 2 * wide)),
        [scalars_spec()] + [anywhere()] * 8,
        anywhere(),
        scratch_shapes=[pltpu.SemaphoreType.DMA((16,))],
    )(place, *pairs)


def side_by_side(ref):
    return jnp.concatenate([ref[head] for head in range(ref.shape[0])], axis=1)


def project_kernel(
    place_ref, scalar_ref, own_ref, other_ref, reward_ref, weight_ref,
    guided_ref, grad_ref, keep_ref, send_ref, held, sems,
):
    rows = own_ref.shape[1]
    half = guided_ref.shape[1]
    heads = own_ref.shape[0]
    blocks = heads // 2
    deep = 2 * HDIM
    copies = []
    for block in range(blocks):
        span = pl.ds(block * deep, deep)
        copies.append(pltpu.make_async_copy(weight_ref.at[span], held.at[span], sems.at[block]))
    for copy in copies:
        copy.start()
    first = place_ref[0] == 0
    gate, strength = scalar_ref[0], scalar_ref[1]
    total = None
    for block in range(blocks):
        head = 2 * block
        columns = jnp.concatenate(
            [
                jnp.concatenate([own_ref[head], own_ref[head + 1]], axis=1),
                jnp.concatenate([other_ref[head], other_ref[head + 1]], axis=1),
            ],
            axis=0,
        )
        copies[block].wait()
        part = jnp.dot(
            columns, held[block * deep : (block + 1) * deep], preferred_element_type=F32
        )
        total = part if total is None else total + part
    branch_out = (gate * total).astype(BF).astype(F32)
    own_out, other_out = branch_out[:rows], branch_out[rows:]
    cond = jnp.where(first, own_out, other_out)
    uncond = jnp.where(first, other_out, own_out)
    guided = uncond + strength * (cond - uncond)
    guided_ref[...] = guided.astype(BF)
    reward = jnp.where(first, reward_ref[:, :half], reward_ref[:, half:]).astype(F32)
    resid = reward - guided
    own_coeff = gate * jnp.where(first, strength, 1.0 - strength)
    other_coeff = gate * jnp.where(first, 1.0 - strength, strength)
    grad = jnp.concatenate([own_coeff * resid, other_coeff * resid], axis=0).astype(BF)
    grad_ref[...] = grad
    for block in range(blocks):
        part = lax.dot_general(
            grad, held[block * deep : (block + 1) * deep], NT, preferred_element_type=F32
        )
        for odd in range(2):
            lanes = part[:, lanes_of(odd)]
            keep_ref[2 * block + odd] = lanes[:rows]
            send_ref[2 * block + odd] = lanes[rows:].astype(BF)


def project(place, scalars, own, other, reward, weight):
    heads, rows, _ = own.shape
    half = reward.shape[1] // 2
    return call(
        project_kernel,
        "project",
        (
            shaped((rows, half)),
            shaped((2 * rows, half)),
            shaped((heads, rows, HDIM), F32),
            shaped((heads, rows, HDIM)),
        ),
        [scalars_spec(), scalars_spec()] + whole(3) + [anywhere()],
        scratch_shapes=[
            pltpu.VMEM(weight.shape, BF),
            pltpu.SemaphoreType.DMA((heads // 2,)),
        ],
    )(place, scalars, own, other, reward, weight)


def weight_kernel(place_ref, own_ref, other_ref, grad_ref, *refs):
    pairs, held, sems = refs[:8], refs[8], refs[9]
    deep, wide = pairs[0].shape[1:]
    grad = grad_ref[...]
    for head in range(own_ref.shape[0]):
        flipped = jnp.concatenate(
            [own_ref[head].astype(F32).T.astype(BF), other_ref[head].astype(F32).T.astype(BF)], axis=1
        )
        part = jnp.dot(flipped, grad, preferred_element_type=F32)
        held[head * HDIM : (head + 1) * HDIM] = part.astype(BF)
    copies = []
    for slot in range(16):
        block, side = piece_place(place_ref, slot)
        rows = pl.ds(pl.multiple_of(block * deep, deep), deep)
        lanes = pl.ds(pl.multiple_of(side * wide, HDIM), wide)
        copies.append(
            pltpu.make_async_copy(
                held.at[rows, lanes], pairs[slot // 2].at[slot % 2], sems.at[slot]
            )
        )
    for copy in copies:
        copy.start()
    for copy in copies:
        copy.wait()


def weight_gradient(place, own, other, grad):
    heads = own.shape[0]
    half = grad.shape[1]
    pair = shaped((2, 2 * HDIM, half // 2))
    return call(
        weight_kernel,
        "weight_gradient",
        (pair,) * 8,
        [scalars_spec()] + whole(3),
        [anywhere()] * 8,
        scratch_shapes=[
            pltpu.VMEM((heads * HDIM, half), BF),
            pltpu.SemaphoreType.DMA((16,)),
        ],
    )(place, own, other, grad)


def add_kernel(keep_ref, got_ref, order_ref, out_ref):
    out_ref[...] = (keep_ref[...] + got_ref[...].astype(F32)).astype(BF)


def add_after(keep, got, order):
    return call(add_kernel, "add_after", shaped(got.shape), whole(2) + [anywhere()])(keep, got, order)


def fill_kernel(here_ref, left_ref, right_ref, packed_ref, order_ref, out_ref, held, sem):
    per = here_ref.shape[1] // HDIM
    deep = EXTRA // per
    total = here_ref[...] + left_ref[...].astype(F32) + right_ref[...].astype(F32)
    total = total.astype(BF)
    for target in range(held.shape[0]):
        for part in range(per):
            held[target, part * deep : (part + 1) * deep, :] = total[
                target * deep : (target + 1) * deep, lanes_of(part)
            ]
    copy = pltpu.make_async_copy(held, out_ref.at[:, pl.ds(0, EXTRA), :], sem)
    copy.start()
    copy.wait()


def fill_extra(here, left, right, packed, order):
    return call(
        fill_kernel,
        "fill_extra",
        shaped(packed.shape),
        whole(3) + [anywhere()] * 2,
        anywhere(),
        input_output_aliases={3: 0},
        scratch_shapes=[
            pltpu.VMEM((packed.shape[0], EXTRA, HDIM), BF),
            pltpu.SemaphoreType.DMA,
        ],
    )(here, left, right, packed, order)


def sum_kernel(in_ref, out_ref):
    sources = in_ref.shape[0]
    deep = out_ref.shape[0]
    per = EXTRA // deep
    for side in range(2):
        for part in range(per):
            rows = slice(part * deep, (part + 1) * deep)
            total = None
            for source in range(sources // 2):
                piece = in_ref[side * (sources // 2) + source, rows, :].astype(F32)
                total = piece if total is None else total + piece
            out_ref[:, lanes_of(side * per + part)] = total


def sum_extra(packed, deep):
    return call(
        sum_kernel,
        "sum_extra",
        shaped((deep, 2 * (EXTRA // deep) * HDIM), F32),
        [extra_spec(packed)],
        grid=(1,),
    )(packed)


def swap_cfg(value):
    return lax.ppermute(value, "cfg", [(0, 1), (1, 0)])


def shift_y(value, step):
    pairs = [(i, (i // 4) * 4 + (i % 4 + step) % 4) for i in range(8)]
    return lax.ppermute(value, "fsdp", pairs)


def shift_x(value, step):
    pairs = []
    for fsdp in range(8):
        for seq in range(16):
            x = ((fsdp // 4) * 2 + seq // 8 + step) % 4
            target = ((x // 2) * 4 + fsdp % 4) * 16 + (x % 2) * 8 + seq % 8
            pairs.append((fsdp * 16 + seq, target))
    return lax.ppermute(value, ("fsdp", "seq"), pairs)


def gather_pairs(piece):
    half = piece.shape[0] // 2
    left = shift_x(piece, 1)
    right = shift_x(piece, -1)
    far_top = shift_x(left[:half], 1)
    far_low = shift_x(right[half:], -1)
    near = jnp.stack([piece, right])
    past = jnp.stack([jnp.concatenate([far_top, far_low]), left])
    near_left, near_right = shift_y(near, 1), shift_y(near, -1)
    past_left, past_right = shift_y(past, 1), shift_y(past, -1)
    near_far = shift_y(near_left, 1)
    past_far = shift_y(past_right, -1)
    return (near, past, near_right, past_right, near_far, past_far, near_left, past_left)


def added(one, two):
    return (one.astype(F32) + two.astype(F32)).astype(BF)


def scatter_pairs(pairs):
    near, past, near_right, past_right, near_far, past_far, near_left, past_left = pairs
    from_left = shift_y(near_far, 1)
    from_right = shift_y(past_far, -1)
    got_past = shift_y(past_right, 1)
    got_near = shift_y(near_left, -1)
    got_near_too = shift_y(added(near_right, from_left), 1)
    got_past_too = shift_y(added(past_left, from_right), -1)
    near = near.astype(F32) + got_near.astype(F32) + got_near_too.astype(F32)
    past = past.astype(F32) + got_past.astype(F32) + got_past_too.astype(F32)
    here, right, far, left = near[0], near[1], past[0].astype(BF), past[1]
    half = far.shape[0] // 2
    got_top = shift_x(far[:half], 1).astype(F32)
    got_low = shift_x(far[half:], -1).astype(F32)
    right = jnp.concatenate([right[:half] + got_top, right[half:]]).astype(BF)
    left = jnp.concatenate([left[:half], left[half:] + got_low]).astype(BF)
    return here, shift_x(right, 1), shift_x(left, -1)


def over_seq(array):
    return lax.all_to_all(array, "seq", split_axis=0, concat_axis=0, tiled=True)


def joined(own, other, first):
    return jnp.where(
        first,
        jnp.concatenate([own, other], axis=1),
        jnp.concatenate([other, own], axis=1),
    )


def places():
    cfg = lax.axis_index("cfg")
    fsdp = lax.axis_index("fsdp")
    x = (fsdp >> 2) * 2 + (lax.axis_index("seq") >> 3)
    y = fsdp & 3
    slots = jnp.arange(16)
    there = (x + (slots & 3)) & 3
    block = (there >> 1) * 4 + ((y + (slots >> 2)) & 3)
    table = jnp.stack([block, there & 1], axis=1).reshape(-1)
    return jnp.concatenate([cfg[None], table]).astype(jnp.int32)


def local(query_act, key_act, value_act, out_weight, reward_dir, guide_index, step_index):
    place = places()
    first_core = place[0] == 0
    moment = step_index[0].astype(F32)
    gate = jnp.cos(0.5 * jnp.pi * (moment + 0.5) / STEPS)
    strength = 1.0 + GUIDE_STEP * guide_index[0].astype(F32)
    scalars = jnp.stack([gate, strength])
    deep = out_weight.shape[0]
    rows = query_act.shape[2]

    first = over_seq(pack_first(place, query_act[0, 0], key_act[0, 0], out_weight))
    value = over_seq(pack_heads(value_act[0, 0]))
    piece = weight_piece(first, deep)
    weight = assemble(place, gather_pairs(piece))
    probs = probabilities(first, piece)
    mixed_h = mix(value, probs)
    mixed = over_seq(mixed_h)
    mixed_other = swap_cfg(mixed)
    guided, grad_out, keep, send = project(
        place, scalars, mixed, mixed_other, reward_dir[0], weight
    )
    parts = weight_gradient(place, mixed, mixed_other, grad_out)
    grad_h = over_seq(add_after(keep, swap_cfg(send), parts[4]))
    sums = scatter_pairs(parts)
    guided_all = joined(guided, swap_cfg(guided), first_core)
    grad_value_h = grad_of_value(grad_h, probs)
    grad_value = over_seq(grad_value_h)
    packed = attend_backward(first, value, mixed_h, grad_h, grad_value_h, probs)
    last = over_seq(fill_extra(*sums, packed, grad_value))
    grad_half = sum_extra(last, deep)
    grad_weight = joined(grad_half, swap_cfg(grad_half), first_core)
    (grad_value,) = unpack_heads(grad_value, 1, rows)
    grad_query, grad_key = unpack_heads(last, 2, rows)
    return (
        guided_all[None],
        grad_query[None, None],
        grad_key[None, None],
        grad_value[None, None],
        grad_weight,
    )


def solution(mesh):
    placed = (
        P("cfg", "fsdp", "seq", None),
        P("cfg", "fsdp", "seq", None),
        P("cfg", "fsdp", "seq", None),
        P(("fsdp", "seq"), None),
        P("fsdp", "seq", None),
        P(),
        P(),
    )
    return jax.shard_map(
        local,
        mesh=mesh,
        in_specs=placed,
        out_specs=(
            P("fsdp", "seq", None),
            P("cfg", "fsdp", "seq", None),
            P("cfg", "fsdp", "seq", None),
            P("cfg", "fsdp", "seq", None),
            P(("fsdp", "seq"), None),
        ),
        check_vma=False,
    )
```

time: 258 us -> 352 us (1.36); the launches traced: 257 us -> 347 us
  Pallas kernels: 44.3 us -> 166 us
  waiting for transfers between devices: 97.8 us -> 73.8 us
  starting transfers between devices: 95.1 us -> 90.8 us
    pallas_call x6 -> x15, Pallas kernels: 44.3 us -> 166 us  [the longest x1 97.2 us: assemble(): call(assemble_kernel, 'assemble', shaped((8 * deep, 2 * wide)), [scalars_...]
    ppermute x14 -> x12, waiting for transfers between devices: 82.2 us -> 6.18 us  [the longest x8 6.17 us: shift_x(): return lax.ppermute(value, ('fsdp', 'seq'), pairs)]
    all_to_all x4 -> x6, waiting for transfers between devices: 6.69 us -> 44.2 us  [over_seq(): return lax.all_to_all(array, 'seq', split_axis=0, concat_axis=0, tiled=True)]
    ppermute x14 -> x12, starting transfers between devices: 56.4 us -> 34.4 us  [the longest x4 21.9 us: swap_cfg(): return lax.ppermute(value, 'cfg', [(0, 1), (1, 0)])]
    ppermute x8 -> x12, waiting for transfers between devices: 8.89 us -> 23.4 us  [shift_y(): return lax.ppermute(value, 'fsdp', pairs)]
    all_to_all x4 -> x6, starting transfers between devices: 30.2 us -> 42.8 us  [over_seq(): return lax.all_to_all(array, 'seq', split_axis=0, concat_axis=0, tiled=True)]
    ppermute x8 -> x12, starting transfers between devices: 8.56 us -> 13.5 us  [shift_y(): return lax.ppermute(value, 'fsdp', pairs)]
    unnamed x36 -> x50, local copies, waits for them, and re-layouts: 5.71 us -> 7.26 us
  transfers between devices with their start and end apart: 26 -> 30, of which waited for: 12 -> 12; matrix products, arithmetic and copies ran while one was open for 4% -> 1% of each run, Pallas kernels for 11% -> 41%
where the time goes in v2:
time: 352 us; the launch traced here: 347 us
  Pallas kernels  166 us (47%)
  starting transfers between devices  90.8 us (26%)
  waiting for transfers between devices  73.8 us (21%)
  local copies, waits for them, and re-layouts  8.27 us (2%)
  other arithmetic  5.46 us (2%)
    pallas_call x1, Pallas kernels, assemble(): call(assemble_kernel, 'assemble', shaped((8 * deep, 2 * wide)), [scalars_...  97.2 us
    all_to_all x6, waiting for transfers between devices, over_seq(): return lax.all_to_all(array, 'seq', split_axis=0, concat_axis=0, tiled=True)  44.2 us
    all_to_all x6, starting transfers between devices, over_seq(): return lax.all_to_all(array, 'seq', split_axis=0, concat_axis=0, tiled=True)  42.8 us
    ppermute x12, waiting for transfers between devices, shift_y(): return lax.ppermute(value, 'fsdp', pairs)  23.4 us
    ppermute x4, starting transfers between devices, swap_cfg(): return lax.ppermute(value, 'cfg', [(0, 1), (1, 0)])  21.9 us
    ppermute x12, starting transfers between devices, shift_y(): return lax.ppermute(value, 'fsdp', pairs)  13.5 us
    pallas_call x1, Pallas kernels, probabilities(): call(probs_kernel, 'probabilities', shaped((length, length)), whole(1) +...  13.3 us
    ppermute x8, starting transfers between devices, shift_x(): return lax.ppermute(value, ('fsdp', 'seq'), pairs)  12.6 us
  transfers between devices with their start and end apart: 30, of which 12 were waited for; matrix products, arithmetic and copies ran while one was open for 1% of the time, Pallas kernels for 41%

profile of v2, /device:TPU:1, one launch (start us, length us, event | category | flops | bytes accessed | tf_op | source)
XLA Modules:
  0.0 346.8 jit_solution(16939539587590436107)
XLA Ops:
  4.0 10.0 %all-to-all-start.1 = ((bf16[16,304,128]{2,1,0:T(8,128)(2,1)}), bf16[16,304,128]{2,1,0:T(8,128)(2,1)S(1)}, u32[]{:S(2)}, u32[]{:S(2)}) async-start(bf16[16,304,128]{2,1,0:T(8,128)(2,1)} %pack_first.1), calls=%async_computation.1 | async-start | bytes 2490368 | tf_op jit(solution)/shard_map/all_to_all | solution.py:539
  15.9 27.5 %all-to-all-done.1.in_ref.first_ref = bf16[16,304,128]{2,1,0:T(8,128)(2,1)S(1)} async-done(((bf16[16,304,128]{2,1,0:T(8,128)(2,1)}), bf16[16,304,128]{2,1,0:T(8,128)(2,1)S(1)}, u32[]{:S(2)}, u32[]{:S(2)}) %all-to-all-start.1) | async-done | bytes 1245216 | tf_op jit(solution)/shard_map/all_to_all | solution.py:539
  43.4 6.4 %all-to-all-start = ((bf16[16,128,128]{2,1,0:T(8,128)(2,1)}), bf16[16,128,128]{2,1,0:T(8,128)(2,1)S(1)}, u32[]{:S(2)}, u32[]{:S(2)}) async-start(bf16[16,128,128]{2,1,0:T(8,128)(2,1)} %pack_heads.1), calls=%async_computation | async-start | bytes 1048576 | tf_op jit(solution)/shard_map/all_to_all | solution.py:539
  51.5 13.3 %probabilities.1.probs_ref = bf16[2048,2048]{1,0:T(8,128)(2,1)} custom-call(bf16[16,304,128]{2,1,0:T(8,128)(2,1)} %copy-done, bf16[256,384]{1,0:T(8,128)(2,1)} %weight_piece.1.order_ref), custom_call_target="tpu_custom_call" | custom-call | tf_op jit(solution)/shard_map/probabilities/pallas_call | solution.py:154
  65.6 8.3 %mix.1.mixed_ref = bf16[16,128,128]{2,1,0:T(8,128)(2,1)} custom-call(bf16[16,128,128]{2,1,0:T(8,128)(2,1)} %copy-done.2, bf16[2048,2048]{1,0:T(8,128)(2,1)} %probabilities.1.probs_ref), custom_call_target="tpu_custom_call" | custom-call | tf_op jit(solution)/shard_map/mix/pallas_call | solution.py:179
  74.0 7.6 %all-to-all-start.2 = ((bf16[16,128,128]{2,1,0:T(8,128)(2,1)}), bf16[16,128,128]{2,1,0:T(8,128)(2,1)S(1)}, u32[]{:S(2)}, u32[]{:S(2)}) async-start(bf16[16,128,128]{2,1,0:T(8,128)(2,1)} %mix.1.mixed_ref), calls=%async_computation.2 | async-start | bytes 1048576 | tf_op jit(solution)/shard_map/all_to_all | solution.py:539
  84.3 4.6 %collective-permute-done.2 = bf16[256,384]{1,0:T(8,128)(2,1)S(1)} collective-permute-done((bf16[256,384]{1,0:T(8,128)(2,1)S(1)}, bf16[256,384]{1,0:T(8,128)(2,1)S(1)}, u32[]{:S(2)}, u32[]{:S(2)}) %collective-permute-start.2) | collective-permute-done | bytes 196640 | tf_op jit(solution)/shard_map/ppermute | solution.py:497
  104.8 3.4 collective-permute-start.9
  114.3 8.4 %collective-permute-done.8.refs_4_ = bf16[2,256,384]{2,1,0:T(8,128)(2,1)S(1)} collective-permute-done((bf16[2,256,384]{2,1,0:T(8,128)(2,1)S(1)}, bf16[2,256,384]{2,1,0:T(8,128)(2,1)S(1)}, u32[]{:S(2)}, u32[]{:S(2)}) %collective-permute-start.8) | collective-permute-done | bytes 393248 | tf_op jit(solution)/shard_map/ppermute | solution.py:487
  124.2 97.2 %assemble.1.weight_ref = bf16[2048,768]{1,0:T(8,128)(2,1)} custom-call(s32[33]{0:T(128)} %pad_add_fusion.1.place_ref, bf16[2,256,384]{2,1,0:T(8,128)(2,1)} %copy-done.8, bf16[2,256,384]{2,1,0:T(8,128)(2,1)} %copy-done.9, bf16[2,256,384]{2,1,0:T(8,128)(2,1)} %copy-done.14, bf16[2,256,384]{2,1,0:T(8,128)(2,1)} %copy-done.13, bf16[2,256,384]{2,1,0:T(8,128)(2,1)} %copy-done.16, ...), custom_call_target="tpu_custom_call" | custom-call | tf_op jit(solution)/shard_map/assemble/pallas_call | solution.py:288
  222.3 6.3 %project.1 = (bf16[128,768]{1,0:T(8,128)(2,1)}, bf16[256,768]{1,0:T(8,128)(2,1)}, f32[16,128,128]{2,1,0:T(8,128)}, bf16[16,128,128]{2,1,0:T(8,128)(2,1)}) custom-call(s32[33]{0:T(128)} %pad_add_fusion.1.place_ref, f32[2]{0:T(128)} %pad_maximum_fusion.4.scalar_ref, bf16[16,128,128]{2,1,0:T(8,128)(2,1)} %copy-done.4, bf16[16,128,128]{2,1,0:T(8,128)(2,1)} %copy-done.6, ...), custom_call_target="tpu_custom_call" | custom-call | tf_op jit(solution)/shard_map/project/pallas_call | solution.py:359
  228.5 4.2 %weight_gradient.1 = (bf16[2,256,384]{2,1,0:T(8,128)(2,1)}, bf16[2,256,384]{2,1,0:T(8,128)(2,1)}, bf16[2,256,384]{2,1,0:T(8,128)(2,1)}, bf16[2,256,384]{2,1,0:T(...) custom-call(s32[33]{0:T(128)} %pad_add_fusion.1.place_ref, ...), custom_call_target="tpu_custom_call" | custom-call | tf_op jit(solution)/shard_map/weight_gradient/pallas_call | solution.py:406
  234.5 4.0 %collective-permute-start.22 = (bf16[16,128,128]{2,1,0:T(8,128)(2,1)S(1)}, bf16[16,128,128]{2,1,0:T(8,128)(2,1)S(1)}, u32[]{:S(2)}, u32[]{:S(2)}) collective-permute-start(bf16[16,128,128]{2,1,0:T(8,128)(2,1)S(1)} %copy-done.24), channel_id=1, source_target_pairs={{0,128},{128,0},{1,129},{129,1},{2,130},{130,2},{3,131},{131,3},{4... | collective-permute-start | bytes 1572872 | tf_op jit(solution)/shard_map/ppermute | solution.py:482
  238.5 3.2 collective-permute-done.16
  246.9 6.8 %all-to-all-start.3 = ((bf16[16,128,128]{2,1,0:T(8,128)(2,1)}), bf16[16,128,128]{2,1,0:T(8,128)(2,1)S(1)}, u32[]{:S(2)}, u32[]{:S(2)}) async-start(bf16[16,128,128]{2,1,0:T(8,128)(2,1)} %add_after.1), calls=%async_computation.3 | async-start | bytes 1048576 | tf_op jit(solution)/shard_map/all_to_all | solution.py:539
  255.3 3.7 %collective-permute-done.15 = bf16[2,256,384]{2,1,0:T(8,128)(2,1)S(1)} collective-permute-done((bf16[2,256,384]{2,1,0:T(8,128)(2,1)}, bf16[2,256,384]{2,1,0:T(8,128)(2,1)S(1)}, u32[]{:S(2)}, u32[]{:S(2)}) %collective-permute-start.15) | collective-permute-done | bytes 393248 | tf_op jit(solution)/shard_map/ppermute | solution.py:487
  266.2 8.3 %grad_of_value.1.order_ref = bf16[16,128,128]{2,1,0:T(8,128)(2,1)} custom-call(bf16[16,128,128]{2,1,0:T(8,128)(2,1)} %copy-done.3, bf16[2048,2048]{1,0:T(8,128)(2,1)} %probabilities.1.probs_ref), custom_call_target="tpu_custom_call" | custom-call | tf_op jit(solution)/shard_map/grad_of_value/pallas_call | solution.py:201
  274.5 5.4 %all-to-all-start.4 = ((bf16[16,128,128]{2,1,0:T(8,128)(2,1)}), bf16[16,128,128]{2,1,0:T(8,128)(2,1)S(1)}, u32[]{:S(2)}, u32[]{:S(2)}) async-start(bf16[16,128,128]{2,1,0:T(8,128)(2,1)} %grad_of_value.1.order_ref), calls=%async_computation.4 | async-start | bytes 1048576 | tf_op jit(solution)/shard_map/all_to_all | solution.py:539
  279.9 3.5 %collective-permute-start.21 = (bf16[256,384]{1,0:T(8,128)(2,1)S(1)}, bf16[256,384]{1,0:T(8,128)(2,1)S(1)}, u32[]{:S(2)}, u32[]{:S(2)}) collective-permute-start(bf16[256,384]{1,0:T(8,128)(2,1)S(1)} %pad_maximum_fusion.3), channel_id=1, source_target_pairs={{0,72},{1,73},{2,74},{3,75},{4,76},{5,77},{6,78},{7,79},{8,0},{9,1... | collective-permute-start | bytes 589832 | tf_op jit(solution)/shard_map/ppermute | solution.py:497
  284.3 12.2 %attend_backward.1.packed_ref = bf16[16,304,128]{2,1,0:T(8,128)(2,1)} custom-call(bf16[16,304,128]{2,1,0:T(8,128)(2,1)} %copy-done, bf16[16,128,128]{2,1,0:T(8,128)(2,1)} %copy-done.2, bf16[16,128,128]{2,1,0:T(8,128)(2,1)} %mix.1.mixed_ref, bf16[16,128,128]{2,1,0:T(8,128)(2,1)} %copy-done.3, bf16[16,128,128]{2,1,0:T(8,128)(2,1)} %grad_of_value.1.order_ref, ...), custom_call_target="tpu_custom_call" | custom-call | tf_op jit(solution)/shard_map/attend_backward/pallas_call | solution.py:250
  300.0 6.6 %all-to-all-start.5 = ((bf16[16,304,128]{2,1,0:T(8,128)(2,1)}), bf16[16,304,128]{2,1,0:T(8,128)(2,1)S(1)}, u32[]{:S(2)}, u32[]{:S(2)}) async-start(bf16[16,304,128]{2,1,0:T(8,128)(2,1)} %fill_extra.1), calls=%async_computation.5 | async-start | bytes 2490368 | tf_op jit(solution)/shard_map/all_to_all | solution.py:539
  306.6 6.9 %collective-permute-start.11 = (bf16[128,768]{1,0:T(8,128)(2,1)S(1)}, bf16[128,768]{1,0:T(8,128)(2,1)S(1)}, u32[]{:S(2)}, u32[]{:S(2)}) collective-permute-start(bf16[128,768]{1,0:T(8,128)(2,1)S(1)} %copy-done.21), channel_id=1, source_target_pairs={{0,128},{128,0},{1,129},{129,1},{2,130},{130,2},{3,131},{131,3},{4... | collective-permute-start | bytes 589832 | tf_op jit(solution)/shard_map/ppermute | solution.py:482
  313.5 16.7 %all-to-all-done.5.in_ref = bf16[16,304,128]{2,1,0:T(8,128)(2,1)S(1)} async-done(((bf16[16,304,128]{2,1,0:T(8,128)(2,1)}), bf16[16,304,128]{2,1,0:T(8,128)(2,1)S(1)}, u32[]{:S(2)}, u32[]{:S(2)}) %all-to-all-start.5) | async-done | bytes 1245216 | tf_op jit(solution)/shard_map/all_to_all | solution.py:539
  332.8 7.9 %collective-permute-start.23 = (f32[16,768]{1,0:T(8,128)}, f32[16,768]{1,0:T(8,128)S(1)}, u32[]{:S(2)}, u32[]{:S(2)}) collective-permute-start(f32[16,768]{1,0:T(8,128)} %sum_extra.1), channel_id=1, source_target_pairs={{0,128},{128,0},{1,129},{129,1},{2,130},{130,2},{3,131},{131,3},{4... | collective-permute-start | bytes 147464 | tf_op jit(solution)/shard_map/ppermute | solution.py:482
  (125 shorter events, 61.9 us)
Async XLA Ops:
  4.0 39.5 %all-to-all-start.1 = ((bf16[16,304,128]{2,1,0:T(8,128)(2,1)}), bf16[16,304,128]{2,1,0:T(8,128)(2,1)S(1)}, u32[]{:S(2)}, u32[]{:S(2)}) async-start(bf16[16,304,128]{2,1,0:T(8,128)(2,1)} %pack_first.1), calls=%async_computation.1 | async-start | bytes 2490368 | tf_op jit(solution)/shard_map/all_to_all | solution.py:539
  43.4 21.4 %all-to-all-start = ((bf16[16,128,128]{2,1,0:T(8,128)(2,1)}), bf16[16,128,128]{2,1,0:T(8,128)(2,1)S(1)}, u32[]{:S(2)}, u32[]{:S(2)}) async-start(bf16[16,128,128]{2,1,0:T(8,128)(2,1)} %pack_heads.1), calls=%async_computation | async-start | bytes 1048576 | tf_op jit(solution)/shard_map/all_to_all | solution.py:539
  74.0 25.2 %all-to-all-start.2 = ((bf16[16,128,128]{2,1,0:T(8,128)(2,1)}), bf16[16,128,128]{2,1,0:T(8,128)(2,1)S(1)}, u32[]{:S(2)}, u32[]{:S(2)}) async-start(bf16[16,128,128]{2,1,0:T(8,128)(2,1)} %mix.1.mixed_ref), calls=%async_computation.2 | async-start | bytes 1048576 | tf_op jit(solution)/shard_map/all_to_all | solution.py:539
  93.3 10.4 %collective-permute-start.7 = (bf16[2,256,384]{2,1,0:T(8,128)(2,1)S(1)}, bf16[2,256,384]{2,1,0:T(8,128)(2,1)S(1)}, u32[]{:S(2)}, u32[]{:S(2)}) collective-permute-start(bf16[2,256,384]{2,1,0:T(8,128)(2,1)S(1)} %pad_maximum_fusion.refs_0_), channel_id=1, source_target_pairs={{0,16},{16,32},{32,48},{48,0},{64,80},{80,96},{96,112},{112,64},{1... | collective-permute-start | bytes 1179656 | tf_op jit(solution)/shard_map/ppermute | solution.py:487
  99.2 122.3 %collective-permute-start = (bf16[16,128,128]{2,1,0:T(8,128)(2,1)S(1)}, bf16[16,128,128]{2,1,0:T(8,128)(2,1)S(1)}, u32[]{:S(2)}, u32[]{:S(2)}) collective-permute-start(bf16[16,128,128]{2,1,0:T(8,128)(2,1)S(1)} %all-to-all-done.2.own_ref), channel_id=1, source_target_pairs={{0,128},{128,0},{1,129},{129,1},{2,130},{130,2},{3,131},{131,3},{4... | collective-permute-start | bytes 1572872 | tf_op jit(solution)/shard_map/ppermute | solution.py:482
  102.2 11.2 %collective-permute-start.5 = (bf16[2,256,384]{2,1,0:T(8,128)(2,1)S(1)}, bf16[2,256,384]{2,1,0:T(8,128)(2,1)S(1)}, u32[]{:S(2)}, u32[]{:S(2)}) collective-permute-start(bf16[2,256,384]{2,1,0:T(8,128)(2,1)S(1)} %pad_maximum_fusion.refs_0_), channel_id=1, source_target_pairs={{0,48},{16,0},{32,16},{48,32},{64,112},{80,64},{96,80},{112,96},{1... | collective-permute-start | bytes 1179656 | tf_op jit(solution)/shard_map/ppermute | solution.py:487
  102.7 11.6 %collective-permute-start.10 = (bf16[2,256,384]{2,1,0:T(8,128)(2,1)S(1)}, bf16[2,256,384]{2,1,0:T(8,128)(2,1)S(1)}, u32[]{:S(2)}, u32[]{:S(2)}) collective-permute-start(bf16[2,256,384]{2,1,0:T(8,128)(2,1)S(1)} %pad_maximum_fusion.1.refs_1_), channel_id=1, source_target_pairs={{0,16},{16,32},{32,48},{48,0},{64,80},{80,96},{96,112},{112,64},{1... | collective-permute-start | bytes 1179656 | tf_op jit(solution)/shard_map/ppermute | solution.py:487
  103.7 19.0 %collective-permute-start.8 = (bf16[2,256,384]{2,1,0:T(8,128)(2,1)S(1)}, bf16[2,256,384]{2,1,0:T(8,128)(2,1)S(1)}, u32[]{:S(2)}, u32[]{:S(2)}) collective-permute-start(bf16[2,256,384]{2,1,0:T(8,128)(2,1)S(1)} %collective-permute-done.7.refs_6_), channel_id=1, source_target_pairs={{0,16},{16,32},{32,48},{48,0},{64,80},{80,96},{96,112},{112,64},{1... | collective-permute-start | bytes 1179656 | tf_op jit(solution)/shard_map/ppermute | solution.py:487
  104.8 17.9 %collective-permute-start.9 = (bf16[2,256,384]{2,1,0:T(8,128)(2,1)S(1)}, bf16[2,256,384]{2,1,0:T(8,128)(2,1)S(1)}, u32[]{:S(2)}, u32[]{:S(2)}) collective-permute-start(bf16[2,256,384]{2,1,0:T(8,128)(2,1)S(1)} %collective-permute-done.6.refs_3_), channel_id=1, source_target_pairs={{0,48},{16,0},{32,16},{48,32},{64,112},{80,64},{96,80},{112,96},{1... | collective-permute-start | bytes 1179656 | tf_op jit(solution)/shard_map/ppermute | solution.py:487
  234.5 9.3 %collective-permute-start.22 = (bf16[16,128,128]{2,1,0:T(8,128)(2,1)S(1)}, bf16[16,128,128]{2,1,0:T(8,128)(2,1)S(1)}, u32[]{:S(2)}, u32[]{:S(2)}) collective-permute-start(bf16[16,128,128]{2,1,0:T(8,128)(2,1)S(1)} %copy-done.24), channel_id=1, source_target_pairs={{0,128},{128,0},{1,129},{129,1},{2,130},{130,2},{3,131},{131,3},{4... | collective-permute-start | bytes 1572872 | tf_op jit(solution)/shard_map/ppermute | solution.py:482
  238.5 15.2 %collective-permute-start.13 = (bf16[2,256,384]{2,1,0:T(8,128)(2,1)}, bf16[2,256,384]{2,1,0:T(8,128)(2,1)S(1)}, u32[]{:S(2)}, u32[]{:S(2)}) collective-permute-start(bf16[2,256,384]{2,1,0:T(8,128)(2,1)} %get-tuple-element.24.order_ref), channel_id=1, source_target_pairs={{0,16},{16,32},{32,48},{48,0},{64,80},{80,96},{96,112},{112,64},{1... | collective-permute-start | bytes 1179656 | tf_op jit(solution)/shard_map/ppermute | solution.py:487
  238.5 20.6 %collective-permute-start.15 = (bf16[2,256,384]{2,1,0:T(8,128)(2,1)}, bf16[2,256,384]{2,1,0:T(8,128)(2,1)S(1)}, u32[]{:S(2)}, u32[]{:S(2)}) collective-permute-start(bf16[2,256,384]{2,1,0:T(8,128)(2,1)} %get-tuple-element.26), channel_id=1, source_target_pairs={{0,16},{16,32},{32,48},{48,0},{64,80},{80,96},{96,112},{112,64},{1... | collective-permute-start | bytes 1179656 | tf_op jit(solution)/shard_map/ppermute | solution.py:487
  242.8 16.3 %collective-permute-start.17 = (bf16[2,256,384]{2,1,0:T(8,128)(2,1)S(1)}, bf16[2,256,384]{2,1,0:T(8,128)(2,1)S(1)}, u32[]{:S(2)}, u32[]{:S(2)}) collective-permute-start(bf16[2,256,384]{2,1,0:T(8,128)(2,1)S(1)} %add_convert_fusion), channel_id=1, source_target_pairs={{0,48},{16,0},{32,16},{48,32},{64,112},{80,64},{96,80},{112,96},{1... | collective-permute-start | bytes 1179656 | tf_op jit(solution)/shard_map/ppermute | solution.py:487
  243.7 17.5 %collective-permute-start.12 = (bf16[2,256,384]{2,1,0:T(8,128)(2,1)}, bf16[2,256,384]{2,1,0:T(8,128)(2,1)}, u32[]{:S(2)}, u32[]{:S(2)}) collective-permute-start(bf16[2,256,384]{2,1,0:T(8,128)(2,1)} %get-tuple-element.22), channel_id=1, source_target_pairs={{0,48},{16,0},{32,16},{48,32},{64,112},{80,64},{96,80},{112,96},{1... | collective-permute-start | bytes 1179656 | tf_op jit(solution)/shard_map/ppermute | solution.py:487
  246.9 18.5 %all-to-all-start.3 = ((bf16[16,128,128]{2,1,0:T(8,128)(2,1)}), bf16[16,128,128]{2,1,0:T(8,128)(2,1)S(1)}, u32[]{:S(2)}, u32[]{:S(2)}) async-start(bf16[16,128,128]{2,1,0:T(8,128)(2,1)} %add_after.1), calls=%async_computation.3 | async-start | bytes 1048576 | tf_op jit(solution)/shard_map/all_to_all | solution.py:539
  253.8 10.4 %collective-permute-start.14 = (bf16[2,256,384]{2,1,0:T(8,128)(2,1)S(1)}, bf16[2,256,384]{2,1,0:T(8,128)(2,1)S(1)}, u32[]{:S(2)}, u32[]{:S(2)}) collective-permute-start(bf16[2,256,384]{2,1,0:T(8,128)(2,1)S(1)} %add_convert_fusion.1), channel_id=1, source_target_pairs={{0,16},{16,32},{32,48},{48,0},{64,80},{80,96},{96,112},{112,64},{1... | collective-permute-start | bytes 1179656 | tf_op jit(solution)/shard_map/ppermute | solution.py:487
  259.3 20.6 %collective-permute-start.20 = (bf16[128,384]{1,0:T(8,128)(2,1)S(1)}, bf16[128,384]{1,0:T(8,128)(2,1)S(1)}, u32[]{:S(2)}, u32[]{:S(2)}) collective-permute-start(bf16[128,384]{1,0:T(8,128)(2,1)S(1)} %get-tuple-element.36), channel_id=1, source_target_pairs={{0,72},{1,73},{2,74},{3,75},{4,76},{5,77},{6,78},{7,79},{8,0},{9,1... | collective-permute-start | bytes 294920 | tf_op jit(solution)/shard_map/ppermute | solution.py:497
  261.2 22.2 %collective-permute-start.18 = (bf16[128,384]{1,0:T(8,128)(2,1)S(1)}, bf16[128,384]{1,0:T(8,128)(2,1)S(1)}, u32[]{:S(2)}, u32[]{:S(2)}) collective-permute-start(bf16[128,384]{1,0:T(8,128)(2,1)S(1)} %get-tuple-element.37), channel_id=1, source_target_pairs={{0,8},{1,9},{2,10},{3,11},{4,12},{5,13},{6,14},{7,15},{8,64},{9,65... | collective-permute-start | bytes 294920 | tf_op jit(solution)/shard_map/ppermute | solution.py:497
  274.5 22.1 %all-to-all-start.4 = ((bf16[16,128,128]{2,1,0:T(8,128)(2,1)}), bf16[16,128,128]{2,1,0:T(8,128)(2,1)S(1)}, u32[]{:S(2)}, u32[]{:S(2)}) async-start(bf16[16,128,128]{2,1,0:T(8,128)(2,1)} %grad_of_value.1.order_ref), calls=%async_computation.4 | async-start | bytes 1048576 | tf_op jit(solution)/shard_map/all_to_all | solution.py:539
  279.9 16.6 %collective-permute-start.21 = (bf16[256,384]{1,0:T(8,128)(2,1)S(1)}, bf16[256,384]{1,0:T(8,128)(2,1)S(1)}, u32[]{:S(2)}, u32[]{:S(2)}) collective-permute-start(bf16[256,384]{1,0:T(8,128)(2,1)S(1)} %pad_maximum_fusion.3), channel_id=1, source_target_pairs={{0,72},{1,73},{2,74},{3,75},{4,76},{5,77},{6,78},{7,79},{8,0},{9,1... | collective-permute-start | bytes 589832 | tf_op jit(solution)/shard_map/ppermute | solution.py:497
  283.5 13.0 %collective-permute-start.19 = (bf16[256,384]{1,0:T(8,128)(2,1)S(1)}, bf16[256,384]{1,0:T(8,128)(2,1)S(1)}, u32[]{:S(2)}, u32[]{:S(2)}) collective-permute-start(bf16[256,384]{1,0:T(8,128)(2,1)S(1)} %pad_maximum_fusion.2), channel_id=1, source_target_pairs={{0,8},{1,9},{2,10},{3,11},{4,12},{5,13},{6,14},{7,15},{8,64},{9,65... | collective-permute-start | bytes 589832 | tf_op jit(solution)/shard_map/ppermute | solution.py:497
  300.0 30.2 %all-to-all-start.5 = ((bf16[16,304,128]{2,1,0:T(8,128)(2,1)}), bf16[16,304,128]{2,1,0:T(8,128)(2,1)S(1)}, u32[]{:S(2)}, u32[]{:S(2)}) async-start(bf16[16,304,128]{2,1,0:T(8,128)(2,1)} %fill_extra.1), calls=%async_computation.5 | async-start | bytes 2490368 | tf_op jit(solution)/shard_map/all_to_all | solution.py:539
  306.6 34.1 %collective-permute-start.11 = (bf16[128,768]{1,0:T(8,128)(2,1)S(1)}, bf16[128,768]{1,0:T(8,128)(2,1)S(1)}, u32[]{:S(2)}, u32[]{:S(2)}) collective-permute-start(bf16[128,768]{1,0:T(8,128)(2,1)S(1)} %copy-done.21), channel_id=1, source_target_pairs={{0,128},{128,0},{1,129},{129,1},{2,130},{130,2},{3,131},{131,3},{4... | collective-permute-start | bytes 589832 | tf_op jit(solution)/shard_map/ppermute | solution.py:482
  332.8 13.3 %collective-permute-start.23 = (f32[16,768]{1,0:T(8,128)}, f32[16,768]{1,0:T(8,128)S(1)}, u32[]{:S(2)}, u32[]{:S(2)}) collective-permute-start(f32[16,768]{1,0:T(8,128)} %sum_extra.1), channel_id=1, source_target_pairs={{0,128},{128,0},{1,129},{129,1},{2,130},{130,2},{3,131},{131,3},{4... | collective-permute-start | bytes 147464 | tf_op jit(solution)/shard_map/ppermute | solution.py:482
  (31 other events, 352.0 us)

commit v3 on v2

v3 whole, which is shorter than its diff:
```python
import functools

import jax
import jax.numpy as jnp
from jax import lax
from jax.experimental import pallas as pl
from jax.experimental.pallas import tpu as pltpu
from jax.sharding import PartitionSpec as P

HDIM = 128
STEPS = 50
GUIDE_STEP = 0.04
LOG2E = 1.4426950408889634
BF = jnp.bfloat16
F32 = jnp.float32
NT = (((1,), (1,)), ((), ()))
VMEM_LIMIT = 20 * 1024 * 1024
EXTRA = 48


def params():
    return pltpu.CompilerParams(vmem_limit_bytes=VMEM_LIMIT)


def whole(count):
    return [pl.BlockSpec(memory_space=pltpu.VMEM) for _ in range(count)]


def anywhere():
    return pl.BlockSpec(memory_space=pl.ANY)


def full(array):
    rank = len(array.shape)
    return pl.BlockSpec(array.shape, lambda i: (0,) * rank)


def scalars_spec():
    return pl.BlockSpec(memory_space=pltpu.SMEM)


def call(kernel, name, out_shape, in_specs, out_specs=None, **kwargs):
    if out_specs is None:
        out_specs = whole(len(out_shape)) if isinstance(out_shape, tuple) else whole(1)[0]
    return pl.pallas_call(
        kernel,
        out_shape=out_shape,
        in_specs=in_specs,
        out_specs=tuple(out_specs) if isinstance(out_shape, tuple) else out_specs,
        compiler_params=params(),
        cost_estimate=pl.CostEstimate(flops=1, bytes_accessed=1, transcendentals=0),
        name=name,
        **kwargs,
    )


def shaped(shape, dtype=BF):
    return jax.ShapeDtypeStruct(shape, dtype)


def kept(shape, dtype=BF):
    return pltpu.VMEM(shape, dtype)


def pin(array):
    return pltpu.with_memory_space_constraint(array, pltpu.VMEM)


def spilled(shape, dtype=BF):
    return pltpu.HBM(shape, dtype)


def out(array):
    return pltpu.with_memory_space_constraint(array, pltpu.HBM)


def ordered(orders):
    return [anywhere()] * len(orders)


def lanes_of(head):
    return slice(head * HDIM, (head + 1) * HDIM)


def pack_first_kernel(place_ref, q_ref, k_ref, w_ref, out_ref):
    rows = q_ref.shape[0]
    deep = w_ref.shape[0]
    first = place_ref[0] == 0
    half = w_ref.shape[1] // 2
    picked = jnp.where(first, w_ref[:, :half], w_ref[:, half:])
    heads = out_ref.shape[0]
    per = EXTRA // deep
    for head in range(heads):
        side = head // (heads // 2)
        for part in range(per):
            out_ref[head, part * deep : (part + 1) * deep, :] = picked[:, lanes_of(side * per + part)]
        out_ref[head, EXTRA : EXTRA + rows, :] = q_ref[:, lanes_of(head)]
        out_ref[head, EXTRA + rows :, :] = k_ref[:, lanes_of(head)]


def pack_first(place, query, key, weight):
    rows, width = query.shape
    return call(
        pack_first_kernel,
        "pack_first",
        kept((width // HDIM, EXTRA + 2 * rows, HDIM)),
        [scalars_spec(), full(query), full(key), full(weight)],
        grid=(1,),
    )(place, out(query), out(key), out(weight))


def pack_kernel(in_ref, out_ref):
    for head in range(out_ref.shape[0]):
        out_ref[head] = in_ref[:, lanes_of(head)]


def pack_heads(array):
    rows, width = array.shape
    return call(pack_kernel, "pack_heads", kept((width // HDIM, rows, HDIM)), [full(array)], grid=(1,))(
        out(array)
    )


def unpack_kernel(in_ref, order_ref, *out_refs):
    rows = out_refs[0].shape[0]
    skip = in_ref.shape[1] - rows * len(out_refs)
    for head in range(in_ref.shape[0]):
        for place, ref in enumerate(out_refs):
            start = skip + place * rows
            ref[:, lanes_of(head)] = in_ref[head, start : start + rows, :]


def unpack_heads(packed, count, rows, order):
    target = shaped((rows, packed.shape[0] * HDIM))
    specs = [full(packed), anywhere()]
    return call(
        unpack_kernel, "unpack_heads", (target,) * count, specs, [full(target)] * count, grid=(1,)
    )(packed, out(order))


def extra_spec(packed):
    return pl.BlockSpec((packed.shape[0], EXTRA, HDIM), lambda i: (0, 0, 0))


def piece_kernel(in_ref, out_ref):
    per = out_ref.shape[1] // HDIM
    deep = EXTRA // per
    for source in range(in_ref.shape[0]):
        for part in range(per):
            out_ref[source * deep : (source + 1) * deep, lanes_of(part)] = in_ref[
                source, part * deep : (part + 1) * deep, :
            ]


def weight_piece(packed, deep):
    return call(
        piece_kernel,
        "weight_piece",
        shaped((packed.shape[0] * deep, EXTRA // deep * HDIM)),
        [extra_spec(packed)],
        grid=(1,),
    )(packed)


CHUNK = 512


def probs_kernel(first_ref, order_ref, probs_ref, held, sems):
    shards, total_rows, _ = first_ref.shape
    rows = (total_rows - EXTRA) // 2
    length = shards * rows
    keys = first_ref[:, EXTRA + rows :, :].reshape(length, HDIM)
    scale = HDIM ** (-0.5) * LOG2E
    take = CHUNK // rows
    copies = []
    for part in range(length // CHUNK):
        here = slice(part * take, (part + 1) * take)
        query = first_ref[here, EXTRA : EXTRA + rows, :].reshape(CHUNK, HDIM)
        scores = lax.dot_general(keys, query, NT, preferred_element_type=F32)
        peak = jnp.max(scores, axis=0, keepdims=True) * scale
        weights = jnp.exp2(scores * scale - peak)
        total = jnp.sum(weights, axis=0, keepdims=True)
        lanes = pl.ds(part * CHUNK, CHUNK)
        held[:, lanes] = (weights * (1.0 / total)).astype(BF)
        copy = pltpu.make_async_copy(held.at[:, lanes], probs_ref.at[:, lanes], sems.at[part])
        copy.start()
        copies.append(copy)
    for copy in copies:
        copy.wait()


def probabilities(first, order):
    shards, total_rows, _ = first.shape
    length = shards * (total_rows - EXTRA) // 2
    return call(
        probs_kernel,
        "probabilities",
        spilled((length, length)),
        whole(1) + [anywhere()],
        anywhere(),
        scratch_shapes=[
            pltpu.VMEM((length, length), BF),
            pltpu.SemaphoreType.DMA((length // CHUNK,)),
        ],
    )(first, order)


def fetch(probs_ref, held, sems, by_rows):
    copies = []
    for part in range(sems.shape[0]):
        span = pl.ds(part * CHUNK, CHUNK)
        where = (span,) if by_rows else (slice(None), span)
        copies.append(pltpu.make_async_copy(probs_ref.at[where], held.at[where], sems.at[part]))
    for copy in copies:
        copy.start()
    return copies


def fetch_scratch(probs):
    return [pltpu.VMEM(probs.shape, BF), pltpu.SemaphoreType.DMA((probs.shape[0] // CHUNK,))]


def mix_kernel(value_ref, probs_ref, *refs):
    out_ref, held, sems = refs[-3:]
    copies = fetch(probs_ref, held, sems, False)
    shards, rows, _ = value_ref.shape
    length = shards * rows
    value_t = value_ref[...].reshape(length, HDIM).astype(F32).T.astype(BF)
    take = CHUNK // rows
    for part in range(length // CHUNK):
        copies[part].wait()
        lanes = slice(part * CHUNK, (part + 1) * CHUNK)
        mixed_t = jnp.dot(value_t, held[:, lanes], preferred_element_type=F32)
        out_ref[part * take : (part + 1) * take] = mixed_t.T.astype(BF).reshape(take, rows, HDIM)


def mix(value, probs, *orders):
    return call(
        mix_kernel,
        "mix",
        kept(value.shape),
        whole(1) + [anywhere()] + ordered(orders),
        scratch_shapes=fetch_scratch(probs),
    )(value, out(probs), *[out(order) for order in orders])


def grad_value_kernel(grad_ref, probs_ref, out_ref, held, sems):
    copies = fetch(probs_ref, held, sems, True)
    shards, rows, _ = grad_ref.shape
    length = shards * rows
    grad = grad_ref[...].reshape(length, HDIM)
    take = CHUNK // rows
    for part in range(length // CHUNK):
        copies[part].wait()
        span = slice(part * CHUNK, (part + 1) * CHUNK)
        result = jnp.dot(held[span, :], grad, preferred_element_type=F32)
        out_ref[part * take : (part + 1) * take] = result.astype(BF).reshape(take, rows, HDIM)


def grad_of_value(grad, probs):
    return call(
        grad_value_kernel,
        "grad_of_value",
        kept(grad.shape),
        whole(1) + [anywhere()],
        scratch_shapes=fetch_scratch(probs),
    )(grad, out(probs))


def backward_kernel(
    first_ref, value_ref, mixed_ref, grad_ref, probs_ref, order_ref, out_ref, query_t, held, sems
):
    copies = fetch(probs_ref, held, sems, True)
    shards, rows, _ = value_ref.shape
    length = shards * rows
    factor = HDIM ** (-0.5)
    grad = grad_ref[...].reshape(length, HDIM)
    mixed = mixed_ref[...].reshape(length, HDIM)
    product = grad.astype(F32) * mixed.astype(F32)
    inner = jnp.sum(product.T, axis=0, keepdims=True)
    query = first_ref[:, EXTRA : EXTRA + rows, :].reshape(length, HDIM)
    chunk = CHUNK // 2
    take = chunk // rows
    for part in range(length // chunk):
        if part % 2 == 0:
            copies[part // 2].wait()
        here = slice(part * take, (part + 1) * take)
        span = slice(part * chunk, (part + 1) * chunk)
        keys = first_ref[here, EXTRA + rows :, :].reshape(chunk, HDIM)
        value = value_ref[here].reshape(chunk, HDIM)
        grad_probs = lax.dot_general(value, grad, NT, preferred_element_type=F32)
        grad_scores = (held[span, :].astype(F32) * (grad_probs - inner)).astype(BF)
        grad_key = jnp.dot(grad_scores, query, preferred_element_type=F32) * factor
        out_ref[here, EXTRA + rows :, :] = grad_key.astype(BF).reshape(take, rows, HDIM)
        keys_t = keys.astype(F32).T.astype(BF)
        piece = jnp.dot(keys_t, grad_scores, preferred_element_type=F32)
        if part == 0:
            query_t[...] = piece
        else:
            query_t[...] += piece
    grad_query = (query_t[...] * factor).T.astype(BF)
    out_ref[:, EXTRA : EXTRA + rows, :] = grad_query.reshape(shards, rows, HDIM)
    out_ref[:, :EXTRA, :] = jnp.zeros((shards, EXTRA, HDIM), BF)


def attend_backward(first, value, mixed, grad, probs, order):
    length = value.shape[0] * value.shape[1]
    return call(
        backward_kernel,
        "attend_backward",
        kept(first.shape),
        [full(first), full(value), full(mixed), full(grad), anywhere(), anywhere()],
        grid=(1,),
        scratch_shapes=[pltpu.VMEM((HDIM, length), F32)] + fetch_scratch(probs),
    )(first, value, mixed, grad, out(probs), out(order))


def piece_place(place_ref, slot):
    block = place_ref[1 + 2 * slot]
    side = place_ref[2 + 2 * slot]
    return block, side


def piece_span(place_ref, slot, deep, wide):
    block, side = piece_place(place_ref, slot)
    rows = pl.ds(pl.multiple_of(block * deep, deep), deep)
    lanes = pl.ds(pl.multiple_of(side * wide, HDIM), wide)
    return rows, lanes


def assemble_kernel(place_ref, *refs):
    pairs, out_ref = refs[:8], refs[8]
    deep, wide = pairs[0].shape[1:]
    for slot in range(16):
        rows, lanes = piece_span(place_ref, slot, deep, wide)
        out_ref[rows, lanes] = pairs[slot // 2][slot % 2]


def assemble(place, pairs):
    _, deep, wide = pairs[0].shape
    return call(
        assemble_kernel,
        "assemble",
        kept((8 * deep, 2 * wide)),
        [scalars_spec()] + [full(pair) for pair in pairs],
        grid=(1,),
    )(place, *[out(pair) for pair in pairs])


def project_kernel(
    place_ref, scalar_ref, own_ref, other_ref, reward_ref, weight_ref,
    guided_ref, grad_ref, keep_ref, send_ref,
):
    rows = own_ref.shape[1]
    half = guided_ref.shape[1]
    heads = own_ref.shape[0]
    blocks = heads // 2
    deep = 2 * HDIM
    first = place_ref[0] == 0
    gate, strength = scalar_ref[0], scalar_ref[1]
    total = None
    for block in range(blocks):
        head = 2 * block
        columns = jnp.concatenate(
            [
                jnp.concatenate([own_ref[head], own_ref[head + 1]], axis=1),
                jnp.concatenate([other_ref[head], other_ref[head + 1]], axis=1),
            ],
            axis=0,
        )
        part = jnp.dot(
            columns, weight_ref[block * deep : (block + 1) * deep], preferred_element_type=F32
        )
        total = part if total is None else total + part
    branch_out = (gate * total).astype(BF).astype(F32)
    own_out, other_out = branch_out[:rows], branch_out[rows:]
    cond = jnp.where(first, own_out, other_out)
    uncond = jnp.where(first, other_out, own_out)
    guided = uncond + strength * (cond - uncond)
    guided_ref[...] = guided.astype(BF)
    reward = jnp.where(first, reward_ref[:, :half], reward_ref[:, half:]).astype(F32)
    resid = reward - guided
    own_coeff = gate * jnp.where(first, strength, 1.0 - strength)
    other_coeff = gate * jnp.where(first, 1.0 - strength, strength)
    grad = jnp.concatenate([own_coeff * resid, other_coeff * resid], axis=0).astype(BF)
    grad_ref[...] = grad
    for block in range(blocks):
        part = lax.dot_general(
            grad, weight_ref[block * deep : (block + 1) * deep], NT, preferred_element_type=F32
        )
        for odd in range(2):
            lanes = part[:, lanes_of(odd)]
            keep_ref[2 * block + odd] = lanes[:rows]
            send_ref[2 * block + odd] = lanes[rows:].astype(BF)


def project(place, scalars, own, other, reward, weight):
    heads, rows, _ = own.shape
    half = reward.shape[1] // 2
    return call(
        project_kernel,
        "project",
        (
            spilled((rows, half)),
            kept((2 * rows, half)),
            kept((heads, rows, HDIM), F32),
            kept((heads, rows, HDIM)),
        ),
        [scalars_spec(), scalars_spec()] + whole(2) + [full(reward)] + whole(1),
        [pl.BlockSpec((rows, half), lambda i: (0, 0))] + whole(3),
        grid=(1,),
    )(place, scalars, pin(own), pin(other), out(reward), pin(weight))


def weight_kernel(place_ref, own_ref, other_ref, grad_ref, *refs):
    pairs, held = refs[:8], refs[8]
    deep, wide = pairs[0].shape[1:]
    grad = grad_ref[...]
    for head in range(own_ref.shape[0]):
        flipped = jnp.concatenate([own_ref[head].T, other_ref[head].T], axis=1)
        part = jnp.dot(flipped, grad, preferred_element_type=F32)
        held[head * HDIM : (head + 1) * HDIM] = part.astype(BF)
    for slot in range(16):
        rows, lanes = piece_span(place_ref, slot, deep, wide)
        pairs[slot // 2][slot % 2] = held[rows, lanes]


def weight_gradient(place, own, other, grad):
    heads = own.shape[0]
    half = grad.shape[1]
    pair = spilled((2, 2 * HDIM, half // 2))
    return call(
        weight_kernel,
        "weight_gradient",
        (pair,) * 8,
        [scalars_spec()] + whole(3),
        [full(pair)] * 8,
        grid=(1,),
        scratch_shapes=[pltpu.VMEM((heads * HDIM, half), BF)],
    )(place, pin(own), pin(other), pin(grad))


def add_kernel(keep_ref, got_ref, order_ref, out_ref):
    out_ref[...] = (keep_ref[...] + got_ref[...].astype(F32)).astype(BF)


def add_after(keep, got, order):
    return call(add_kernel, "add_after", kept(got.shape), whole(2) + [anywhere()])(
        pin(keep), pin(got), out(order)
    )


def hold_kernel(in_ref, *refs):
    del refs


def hold(array, *orders):
    return call(
        hold_kernel,
        "hold",
        kept(array.shape),
        whole(1) + ordered(orders),
        input_output_aliases={0: 0},
    )(pin(array), *[out(order) for order in orders])


def fill_kernel(here_ref, left_ref, right_ref, far_ref, packed_ref, first_order, second_order, out_ref):
    per = here_ref.shape[1] // HDIM
    deep = EXTRA // per
    total = here_ref[...] + left_ref[...].astype(F32) + right_ref[...].astype(F32)
    total = (total + far_ref[...].astype(F32)).astype(BF)
    for target in range(out_ref.shape[0]):
        for part in range(per):
            out_ref[target, part * deep : (part + 1) * deep, :] = total[
                target * deep : (target + 1) * deep, lanes_of(part)
            ]


def fill_extra(here, left, right, far, packed, first_order, second_order):
    return call(
        fill_kernel,
        "fill_extra",
        kept(packed.shape),
        [full(array) for array in (here, left, right, far)] + whole(1) + [anywhere()] * 2,
        whole(1)[0],
        grid=(1,),
        input_output_aliases={4: 0},
    )(out(here), out(left), out(right), out(far), pin(packed), out(first_order), out(second_order))


def sum_kernel(in_ref, out_ref):
    sources = in_ref.shape[0]
    deep = out_ref.shape[0]
    per = EXTRA // deep
    for side in range(2):
        for part in range(per):
            rows = slice(part * deep, (part + 1) * deep)
            total = None
            for source in range(sources // 2):
                piece = in_ref[side * (sources // 2) + source, rows, :].astype(F32)
                total = piece if total is None else total + piece
            out_ref[:, lanes_of(side * per + part)] = total


def sum_extra(packed, deep):
    return call(
        sum_kernel,
        "sum_extra",
        shaped((deep, 2 * (EXTRA // deep) * HDIM), F32),
        [extra_spec(packed)],
        grid=(1,),
    )(packed)


def swap_cfg(value):
    return lax.ppermute(value, "cfg", [(0, 1), (1, 0)])


def shift_y(value, step):
    pairs = [(i, (i // 4) * 4 + (i % 4 + step) % 4) for i in range(8)]
    return lax.ppermute(value, "fsdp", pairs)


def shift_x(value, step):
    pairs = []
    for fsdp in range(8):
        for seq in range(16):
            x = ((fsdp // 4) * 2 + seq // 8 + step) % 4
            target = ((x // 2) * 4 + fsdp % 4) * 16 + (x % 2) * 8 + seq % 8
            pairs.append((fsdp * 16 + seq, target))
    return lax.ppermute(value, ("fsdp", "seq"), pairs)


def gather_pairs(piece):
    right, left, far = shift_x(piece, -1), shift_x(piece, 1), shift_x(piece, 2)
    near = jnp.stack([piece, right])
    past = jnp.stack([far, left])
    near_left, near_right = shift_y(near, 1), shift_y(near, -1)
    past_left, past_right = shift_y(past, 1), shift_y(past, -1)
    near_far = shift_y(near_left, 1)
    past_far = shift_y(past_right, -1)
    return (near, past, near_right, past_right, near_far, past_far, near_left, past_left)


def plus(one, two):
    return one[...].astype(F32) + two[...].astype(F32)


def pair_kernel(*refs):
    near, past, near_right, past_left, from_left, from_right, got_past, got_near = refs[:8]
    near_out, past_out, right_out, left_out = refs[9:]
    right_out[...] = plus(near_right, from_left).astype(BF)
    left_out[...] = plus(past_left, from_right).astype(BF)
    near_out[...] = plus(near, got_near)
    past_out[...] = plus(past, got_past)


def pair_sums(pairs, order):
    shape = pairs[0].shape
    outs = (spilled(shape, F32),) * 2 + (spilled(shape),) * 2
    return call(
        pair_kernel,
        "pair_sums",
        outs,
        [full(pair) for pair in pairs] + [anywhere()],
        [full(target) for target in outs],
        grid=(1,),
    )(*[out(pair) for pair in pairs], out(order))


def ring_kernel(near, near_got, past, past_got, here_ref, right_ref, far_ref, left_ref):
    outs = ((here_ref, right_ref), (far_ref, left_ref))
    for refs, targets in zip(((near, near_got), (past, past_got)), outs):
        for slot, target in enumerate(targets):
            target[...] = (refs[0][slot] + refs[1][slot].astype(F32)).astype(target.dtype)


def ring_sums(*pairs):
    shape = pairs[0].shape[1:]
    outs = (spilled(shape, F32),) + (spilled(shape),) * 3
    return call(
        ring_kernel,
        "ring_sums",
        outs,
        [full(pair) for pair in pairs],
        [full(target) for target in outs],
        grid=(1,),
    )(*[out(pair) for pair in pairs])


def scatter_y(parts, order):
    near, past, near_right, past_right, near_far, past_far, near_left, past_left = parts
    received = (
        shift_y(near_far, 1),
        shift_y(past_far, -1),
        shift_y(past_right, 1),
        shift_y(near_left, -1),
    )
    near, past, right, left = pair_sums((near, past, near_right, past_left) + received, order)
    return near, shift_y(right, 1), past, shift_y(left, -1)


def scatter_x(near, near_got, past, past_got):
    here, right, far, left = ring_sums(near, near_got, past, past_got)
    return here, shift_x(right, 1), shift_x(left, -1), shift_x(far, 2)


def over_seq(array):
    return lax.all_to_all(array, "seq", split_axis=0, concat_axis=0, tiled=True)


def join_kernel(place_ref, own_ref, other_ref, order_ref, out_ref):
    first = place_ref[0] == 0
    half = own_ref.shape[1]
    out_ref[:, :half] = jnp.where(first, own_ref[...], other_ref[...])
    out_ref[:, half:] = jnp.where(first, other_ref[...], own_ref[...])


def joined(place, own, other, order):
    rows, half = own.shape
    return call(
        join_kernel,
        "joined",
        shaped((rows, 2 * half), own.dtype),
        [scalars_spec(), full(own), full(other), anywhere()],
        pl.BlockSpec((rows, 2 * half), lambda i: (0, 0)),
        grid=(1,),
    )(place, out(own), out(other), out(order))


def places():
    cfg = lax.axis_index("cfg")
    fsdp = lax.axis_index("fsdp")
    x = (fsdp >> 2) * 2 + (lax.axis_index("seq") >> 3)
    y = fsdp & 3
    slots = jnp.arange(16)
    there = (x + (slots & 3)) & 3
    block = (there >> 1) * 4 + ((y + (slots >> 2)) & 3)
    table = jnp.stack([block, there & 1], axis=1).reshape(-1)
    return jnp.concatenate([cfg[None], table]).astype(jnp.int32)


def local(query_act, key_act, value_act, out_weight, reward_dir, guide_index, step_index):
    place = places()
    moment = step_index[0].astype(F32)
    gate = jnp.cos(0.5 * jnp.pi * (moment + 0.5) / STEPS)
    strength = 1.0 + GUIDE_STEP * guide_index[0].astype(F32)
    scalars = jnp.stack([gate, strength])
    deep = out_weight.shape[0]
    rows = query_act.shape[2]

    first = over_seq(pack_first(place, query_act[0, 0], key_act[0, 0], out_weight))
    value = over_seq(pack_heads(value_act[0, 0]))
    piece = weight_piece(first, deep)
    pairs = gather_pairs(piece)
    weight = assemble(place, pairs)
    probs = probabilities(first, piece)
    mixed_h = mix(value, probs, pairs[1], pairs[2], pairs[6])
    mixed = hold(over_seq(mixed_h), pairs[3], pairs[4], pairs[5], pairs[7])
    mixed_other = swap_cfg(mixed)
    guided, grad_out, keep, send = project(
        place, scalars, mixed, mixed_other, reward_dir[0], weight
    )
    parts = weight_gradient(place, mixed, mixed_other, grad_out)
    grad_mixed = add_after(keep, swap_cfg(send), parts[4])
    grad_h = over_seq(grad_mixed)
    grad_value_h = grad_of_value(grad_h, probs)
    grad_value = over_seq(grad_value_h)
    ring = scatter_y(parts, grad_value_h)
    guided_all = joined(place, guided, swap_cfg(guided), grad_value_h)
    packed = attend_backward(first, value, mixed_h, grad_h, probs, grad_value_h)
    last = over_seq(fill_extra(*scatter_x(*ring), packed, grad_value, guided_all))
    grad_half = sum_extra(last, deep)
    grad_weight = joined(place, grad_half, swap_cfg(grad_half), grad_half)
    (grad_value,) = unpack_heads(grad_value, 1, rows, place)
    grad_query, grad_key = unpack_heads(last, 2, rows, grad_value)
    return (
        guided_all[None],
        grad_query[None, None],
        grad_key[None, None],
        grad_value[None, None],
        grad_weight,
    )


def solution(mesh):
    placed = (
        P("cfg", "fsdp", "seq", None),
        P("cfg", "fsdp", "seq", None),
        P("cfg", "fsdp", "seq", None),
        P(("fsdp", "seq"), None),
        P("fsdp", "seq", None),
        P(),
        P(),
    )
    return jax.shard_map(
        local,
        mesh=mesh,
        in_specs=placed,
        out_specs=(
            P("fsdp", "seq", None),
            P("cfg", "fsdp", "seq", None),
            P("cfg", "fsdp", "seq", None),
            P("cfg", "fsdp", "seq", None),
            P(("fsdp", "seq"), None),
        ),
        check_vma=False,
    )
```

time: 352 us -> 247 us (0.70)
  Pallas kernels: 166 us -> 57.9 us
  blocking collectives: 0 us -> 33.3 us
  waiting for transfers between devices: 73.8 us -> 61.2 us
  starting transfers between devices: 90.8 us -> 79.2 us
  other arithmetic: 5.46 us -> 1.01 us
    pallas_call x12 -> x17, Pallas kernels: 159 us -> 54.6 us  [the longest x1 9.49 us: probabilities(): call(probs_kernel, 'probabilities', spilled((length, length)), whole(1) +...]
    all_to_all x0 -> x1, blocking collectives: none -> 33.3 us  [over_seq(): return lax.all_to_all(array, 'seq', split_axis=0, concat_axis=0, tiled=True)]
    ppermute x4, starting transfers between devices: 21.9 us -> 12.3 us  [swap_cfg(): return lax.ppermute(value, 'cfg', [(0, 1), (1, 0)])]
    all_to_all x6 -> x5, waiting for transfers between devices: 44.2 us -> 35.3 us  [over_seq(): return lax.all_to_all(array, 'seq', split_axis=0, concat_axis=0, tiled=True)]
    ppermute x8 -> x6, starting transfers between devices: 12.6 us -> 10.5 us  [shift_x(): return lax.ppermute(value, ('fsdp', 'seq'), pairs)]
    all_to_all x6 -> x5, starting transfers between devices: 42.8 us -> 40.9 us  [over_seq(): return lax.all_to_all(array, 'seq', split_axis=0, concat_axis=0, tiled=True)]
    unnamed x50 -> x48, local copies, waits for them, and re-layouts: 7.26 us -> 6.69 us
  transfers between devices with their start and end apart: 30 -> 27, of which waited for: 12 -> 7; matrix products, arithmetic and copies ran while one was open for 1% -> 0% of each run, Pallas kernels for 41% -> 18%
where the time goes in v3:
time: 247 us; the launch traced here: 242 us
  starting transfers between devices  79.2 us (32%)
  waiting for transfers between devices  61.2 us (25%)
  Pallas kernels  57.9 us (23%)
  blocking collectives  33.3 us (13%)
  local copies, waits for them, and re-layouts  6.86 us (3%)
  between operations  2.85 us (1%)
    all_to_all x5, starting transfers between devices, over_seq(): return lax.all_to_all(array, 'seq', split_axis=0, concat_axis=0, tiled=True)  40.9 us
    all_to_all x5, waiting for transfers between devices, over_seq(): return lax.all_to_all(array, 'seq', split_axis=0, concat_axis=0, tiled=True)  35.3 us
    all_to_all x1, blocking collectives, over_seq(): return lax.all_to_all(array, 'seq', split_axis=0, concat_axis=0, tiled=True)  33.3 us
    ppermute x12, waiting for transfers between devices, shift_y(): return lax.ppermute(value, 'fsdp', pairs)  21.5 us
    ppermute x12, starting transfers between devices, shift_y(): return lax.ppermute(value, 'fsdp', pairs)  15.5 us
    ppermute x4, starting transfers between devices, swap_cfg(): return lax.ppermute(value, 'cfg', [(0, 1), (1, 0)])  12.3 us
    ppermute x6, starting transfers between devices, shift_x(): return lax.ppermute(value, ('fsdp', 'seq'), pairs)  10.5 us
    pallas_call x1, Pallas kernels, probabilities(): call(probs_kernel, 'probabilities', spilled((length, length)), whole(1) +...  9.49 us
  transfers between devices with their start and end apart: 27, of which 7 were waited for; matrix products, arithmetic and copies ran while one was open for 0% of the time, Pallas kernels for 18%

profile of v3, /device:TPU:1, one launch (start us, length us, event | category | flops | bytes accessed | tf_op | source)
XLA Modules:
  0.0 242.3 jit_solution(6210088205522243852)
XLA Ops:
  3.4 10.0 %all-to-all-start.1 = ((bf16[16,304,128]{2,1,0:T(8,128)(2,1)}), bf16[16,304,128]{2,1,0:T(8,128)(2,1)S(1)}, u32[]{:S(2)}, u32[]{:S(2)}) async-start(bf16[16,304,128]{2,1,0:T(8,128)(2,1)} %pack_first.1), calls=%async_computation.1 | async-start | bytes 2490368 | tf_op jit(solution)/shard_map/all_to_all | solution.py:609
  15.4 27.5 %all-to-all-done.1.in_ref.first_ref = bf16[16,304,128]{2,1,0:T(8,128)(2,1)S(1)} async-done(((bf16[16,304,128]{2,1,0:T(8,128)(2,1)}), bf16[16,304,128]{2,1,0:T(8,128)(2,1)S(1)}, u32[]{:S(2)}, u32[]{:S(2)}) %all-to-all-start.1) | async-done | bytes 1245216 | tf_op jit(solution)/shard_map/all_to_all | solution.py:609
  42.9 6.4 %all-to-all-start = ((bf16[16,128,128]{2,1,0:T(8,128)(2,1)}), bf16[16,128,128]{2,1,0:T(8,128)(2,1)S(1)}, u32[]{:S(2)}, u32[]{:S(2)}) async-start(bf16[16,128,128]{2,1,0:T(8,128)(2,1)} %pack_heads.1), calls=%async_computation | async-start | bytes 1048576 | tf_op jit(solution)/shard_map/all_to_all | solution.py:609
  49.4 2.7 %collective-permute-start.2 = (bf16[256,384]{1,0:T(8,128)(2,1)S(1)}, bf16[256,384]{1,0:T(8,128)(2,1)S(1)}, u32[]{:S(2)}, u32[]{:S(2)}) collective-permute-start(bf16[256,384]{1,0:T(8,128)(2,1)S(1)} %weight_piece.1.order_ref), channel_id=1, source_target_pairs={{0,72},{1,73},{2,74},{3,75},{4,76},{5,77},{6,78},{7,79},{8,0},{9,1... | collective-permute-start | bytes 589832 | tf_op jit(solution)/shard_map/ppermute | solution.py:531
  52.1 4.4 %collective-permute-done.2 = bf16[256,384]{1,0:T(8,128)(2,1)S(1)} collective-permute-done((bf16[256,384]{1,0:T(8,128)(2,1)S(1)}, bf16[256,384]{1,0:T(8,128)(2,1)S(1)}, u32[]{:S(2)}, u32[]{:S(2)}) %collective-permute-start.2) | collective-permute-done | bytes 196640 | tf_op jit(solution)/shard_map/ppermute | solution.py:531
  62.4 9.5 %probabilities.1.probs_ref = bf16[2048,2048]{1,0:T(8,128)(2,1)} custom-call(bf16[16,304,128]{2,1,0:T(8,128)(2,1)S(1)} %all-to-all-done.1.in_ref.first_ref, bf16[256,384]{1,0:T(8,128)(2,1)S(1)} %weight_piece.1.order_ref), custom_call_target="tpu_custom_call" | custom-call | flops 1 | bytes 1 | tf_op jit(solution)/shard_map/probabilities/pallas_call | solution.py:195
  74.2 5.0 %mix.1.mixed_ref = bf16[16,128,128]{2,1,0:T(8,128)(2,1)} custom-call(bf16[16,128,128]{2,1,0:T(8,128)(2,1)S(1)} %all-to-all-done.value_ref, bf16[2048,2048]{1,0:T(8,128)(2,1)} %probabilities.1.probs_ref, bf16[2,256,384]{2,1,0:T(8,128)(2,1)} %pad_maximum_fusion.refs_0_.refs_1_, bf16[2,256,384]{2,1,0:T(8,128)(2,1)} %copy-done.13, bf16[2,256,384]{2,1,0:T(8,128)(2,1)} %copy-done.12), custom_call_target="tpu_custom_call" | custom-call | flops 1 | bytes 1 | tf_op jit(solution)/shard_map/mix/pallas_call | solution.py:238
  79.2 10.3 %all-to-all-start.2 = ((bf16[16,128,128]{2,1,0:T(8,128)(2,1)}), bf16[16,128,128]{2,1,0:T(8,128)(2,1)S(1)}, u32[]{:S(2)}, u32[]{:S(2)}) async-start(bf16[16,128,128]{2,1,0:T(8,128)(2,1)} %mix.1.mixed_ref), calls=%async_computation.2 | async-start | bytes 1048576 | tf_op jit(solution)/shard_map/all_to_all | solution.py:609
  91.0 6.9 %collective-permute-done.5.refs_0_.refs_3_ = bf16[2,256,384]{2,1,0:T(8,128)(2,1)S(1)} collective-permute-done((bf16[2,256,384]{2,1,0:T(8,128)(2,1)S(1)}, bf16[2,256,384]{2,1,0:T(8,128)(2,1)S(1)}, u32[]{:S(2)}, u32[]{:S(2)}) %collective-permute-start.5) | collective-permute-done | bytes 393248 | tf_op jit(solution)/shard_map/ppermute | solution.py:521
  100.6 4.9 %collective-permute-done.7.refs_2_.refs_5_ = bf16[2,256,384]{2,1,0:T(8,128)(2,1)S(1)} collective-permute-done((bf16[2,256,384]{2,1,0:T(8,128)(2,1)S(1)}, bf16[2,256,384]{2,1,0:T(8,128)(2,1)S(1)}, u32[]{:S(2)}, u32[]{:S(2)}) %collective-permute-start.7) | collective-permute-done | bytes 393248 | tf_op jit(solution)/shard_map/ppermute | solution.py:521
  105.5 3.6 %collective-permute-done.6.refs_1_.refs_4_ = bf16[2,256,384]{2,1,0:T(8,128)(2,1)} collective-permute-done((bf16[2,256,384]{2,1,0:T(8,128)(2,1)}, bf16[2,256,384]{2,1,0:T(8,128)(2,1)}, u32[]{:S(2)}, u32[]{:S(2)}) %collective-permute-start.6) | collective-permute-done | bytes 393248 | tf_op jit(solution)/shard_map/ppermute | solution.py:521
  109.2 4.6 %collective-permute-start.9 = (bf16[16,128,128]{2,1,0:T(8,128)(2,1)S(1)}, bf16[16,128,128]{2,1,0:T(8,128)(2,1)S(1)}, u32[]{:S(2)}, u32[]{:S(2)}) collective-permute-start(bf16[16,128,128]{2,1,0:T(8,128)(2,1)S(1)} %hold.1.own_ref), channel_id=1, source_target_pairs={{0,128},{128,0},{1,129},{129,1},{2,130},{130,2},{3,131},{131,3},{4... | collective-permute-start | bytes 1572872 | tf_op jit(solution)/shard_map/ppermute | solution.py:516
  117.4 3.8 %project.1 = (bf16[128,768]{1,0:T(8,128)(2,1)}, bf16[256,768]{1,0:T(8,128)(2,1)S(1)}, f32[16,128,128]{2,1,0:T(8,128)S(1)}, bf16[16,128,128]{2,1,0:T(8,128)(2,1)S(1)}) custom-call(s32[33]{0:T(128)S(1)} %pad_add_fusion.1.place_ref.order_ref, f32[2]{0:T(128)S(1)} %pad_maximum_fusion.2.scalar_ref, bf16[16,128,128]{2,1,0:T(8,128)(2,1)S(1)} %hold.1.own_ref, ...), custom_call_target="tpu_custom_call" | custom-call | flops 1 | bytes 1 | tf_op jit(solution)/shard_map/project/pallas_call | solution.py:400
  121.2 3.2 %weight_gradient.1 = (bf16[2,256,384]{2,1,0:T(8,128)(2,1)}, bf16[2,256,384]{2,1,0:T(8,128)(2,1)}, bf16[2,256,384]{2,1,0:T(8,128)(2,1)}, bf16[2,256,384]{2,1,0:T(...) custom-call(s32[33]{0:T(128)S(1)} %pad_add_fusion.1.place_ref.order_, ...), custom_call_target="tpu_custom_call" | custom-call | flops 1 | bytes 1 | tf_op jit(solution)/shard_map/weight_gradient/pallas_call | solution.py:432
  125.3 7.4 %all-to-all-start.3 = ((bf16[16,128,128]{2,1,0:T(8,128)(2,1)}), bf16[16,128,128]{2,1,0:T(8,128)(2,1)S(1)}, u32[]{:S(2)}, u32[]{:S(2)}) async-start(bf16[16,128,128]{2,1,0:T(8,128)(2,1)} %add_after.1), calls=%async_computation.3 | async-start | bytes 1048576 | tf_op jit(solution)/shard_map/all_to_all | solution.py:609
  138.1 7.8 %all-to-all-done.3.grad_ref = bf16[16,128,128]{2,1,0:T(8,128)(2,1)S(1)} async-done(((bf16[16,128,128]{2,1,0:T(8,128)(2,1)}), bf16[16,128,128]{2,1,0:T(8,128)(2,1)S(1)}, u32[]{:S(2)}, u32[]{:S(2)}) %all-to-all-start.3) | async-done | bytes 524320 | tf_op jit(solution)/shard_map/all_to_all | solution.py:609
  145.9 7.3 %grad_of_value.1.order_ref.refs_8_ = bf16[16,128,128]{2,1,0:T(8,128)(2,1)} custom-call(bf16[16,128,128]{2,1,0:T(8,128)(2,1)S(1)} %all-to-all-done.3.grad_ref, bf16[2048,2048]{1,0:T(8,128)(2,1)} %probabilities.1.probs_ref), custom_call_target="tpu_custom_call" | custom-call | flops 1 | bytes 1 | tf_op jit(solution)/shard_map/grad_of_value/pallas_call | solution.py:261
  153.2 6.7 %all-to-all-start.4 = ((bf16[16,128,128]{2,1,0:T(8,128)(2,1)}), bf16[16,128,128]{2,1,0:T(8,128)(2,1)S(1)}, u32[]{:S(2)}, u32[]{:S(2)}) async-start(bf16[16,128,128]{2,1,0:T(8,128)(2,1)} %grad_of_value.1.order_ref.refs_8_), calls=%async_computation.4 | async-start | bytes 1048576 | tf_op jit(solution)/shard_map/all_to_all | solution.py:609
  160.9 3.3 %pair_sums.1 = (f32[2,256,384]{2,1,0:T(8,128)}, f32[2,256,384]{2,1,0:T(8,128)}, bf16[2,256,384]{2,1,0:T(8,128)(2,1)}, bf16[2,256,384]{2,1,0:T(8,128)(2,1)}) custom-call(bf16[2,256,384]{2,1,0:T(8,128)(2,1)} %get-tuple-element.32.refs_0_, bf16[2,256,384]{2,1,0:T(8,128)(2,1)} %get-tuple-element.33.refs_1_, bf16[2,256,384]{2,1,0:T(8,128)(2,1)} %get-tuple-element.34.refs_2_, ...), custom_call_target="tpu_custom_call" | custom-call | flops 1 | bytes 1 | tf_op jit(solution)/shard_map/pair_sums/pallas_call | solution.py:561
  164.3 2.9 %collective-permute-start.17 = (bf16[2,256,384]{2,1,0:T(8,128)(2,1)}, bf16[2,256,384]{2,1,0:T(8,128)(2,1)S(1)}, u32[]{:S(2)}, u32[]{:S(2)}) collective-permute-start(bf16[2,256,384]{2,1,0:T(8,128)(2,1)} %get-tuple-element.42), channel_id=1, source_target_pairs={{0,48},{16,0},{32,16},{48,32},{64,112},{80,64},{96,80},{112,96},{1... | collective-permute-start | bytes 1179656 | tf_op jit(solution)/shard_map/ppermute | solution.py:521
  169.0 6.0 %collective-permute-done.16.near_got = bf16[2,256,384]{2,1,0:T(8,128)(2,1)S(1)} collective-permute-done((bf16[2,256,384]{2,1,0:T(8,128)(2,1)}, bf16[2,256,384]{2,1,0:T(8,128)(2,1)S(1)}, u32[]{:S(2)}, u32[]{:S(2)}) %collective-permute-start.16) | collective-permute-done | bytes 393248 | tf_op jit(solution)/shard_map/ppermute | solution.py:521
  183.4 8.9 %attend_backward.1.packed_ref = bf16[16,304,128]{2,1,0:T(8,128)(2,1)S(1)} custom-call(bf16[16,304,128]{2,1,0:T(8,128)(2,1)S(1)} %all-to-all-done.1.in_ref.first_ref, bf16[16,128,128]{2,1,0:T(8,128)(2,1)S(1)} %copy-done.3, bf16[16,128,128]{2,1,0:T(8,128)(2,1)} %mix.1.mixed_ref, bf16[16,128,128]{2,1,0:T(8,128)(2,1)S(1)} %all-to-all-done.3.grad_ref, ...), custom_call_target="tpu_custom_call" | custom-call | flops 1 | bytes 1 | tf_op jit(solution)/shard_map/attend_backward/pallas_call | solution.py:308
  198.3 33.3 %all_to_all.30.in_ref = bf16[16,304,128]{2,1,0:T(8,128)(2,1)S(1)} all-to-all(bf16[16,304,128]{2,1,0:T(8,128)(2,1)S(1)} %fill_extra.1), channel_id=1, replica_groups=mesh['cfg'=2,'fsdp'=8,'seq'=16] {'seq'}, dimensions={0} | all-to-all | bytes 2490368 | tf_op jit(solution)/shard_map/all_to_all | solution.py:609
  231.7 5.9 %collective-permute-start.21 = (f32[16,768]{1,0:T(8,128)S(1)}, f32[16,768]{1,0:T(8,128)S(1)}, u32[]{:S(2)}, u32[]{:S(2)}) collective-permute-start(f32[16,768]{1,0:T(8,128)S(1)} %sum_extra.1.own_ref.order_ref), channel_id=1, source_target_pairs={{0,128},{128,0},{1,129},{129,1},{2,130},{130,2},{3,131},{131,3},{4... | collective-permute-start | bytes 147464 | tf_op jit(solution)/shard_map/ppermute | solution.py:516
  (107 shorter events, 47.0 us)
Async XLA Ops:
  3.4 39.5 %all-to-all-start.1 = ((bf16[16,304,128]{2,1,0:T(8,128)(2,1)}), bf16[16,304,128]{2,1,0:T(8,128)(2,1)S(1)}, u32[]{:S(2)}, u32[]{:S(2)}) async-start(bf16[16,304,128]{2,1,0:T(8,128)(2,1)} %pack_first.1), calls=%async_computation.1 | async-start | bytes 2490368 | tf_op jit(solution)/shard_map/all_to_all | solution.py:609
  42.9 29.8 %all-to-all-start = ((bf16[16,128,128]{2,1,0:T(8,128)(2,1)}), bf16[16,128,128]{2,1,0:T(8,128)(2,1)S(1)}, u32[]{:S(2)}, u32[]{:S(2)}) async-start(bf16[16,128,128]{2,1,0:T(8,128)(2,1)} %pack_heads.1), calls=%async_computation | async-start | bytes 1048576 | tf_op jit(solution)/shard_map/all_to_all | solution.py:609
  56.6 16.1 %collective-permute-start.4 = (bf16[2,256,384]{2,1,0:T(8,128)(2,1)S(1)}, bf16[2,256,384]{2,1,0:T(8,128)(2,1)S(1)}, u32[]{:S(2)}, u32[]{:S(2)}) collective-permute-start(bf16[2,256,384]{2,1,0:T(8,128)(2,1)S(1)} %pad_maximum_fusion.1.refs_0_), channel_id=1, source_target_pairs={{0,16},{16,32},{32,48},{48,0},{64,80},{80,96},{96,112},{112,64},{1... | collective-permute-start | bytes 1179656 | tf_op jit(solution)/shard_map/ppermute | solution.py:521
  58.0 14.8 %collective-permute-start.3 = (bf16[2,256,384]{2,1,0:T(8,128)(2,1)S(1)}, bf16[2,256,384]{2,1,0:T(8,128)(2,1)S(1)}, u32[]{:S(2)}, u32[]{:S(2)}) collective-permute-start(bf16[2,256,384]{2,1,0:T(8,128)(2,1)S(1)} %pad_maximum_fusion.1.refs_0_), channel_id=1, source_target_pairs={{0,48},{16,0},{32,16},{48,32},{64,112},{80,64},{96,80},{112,96},{1... | collective-permute-start | bytes 1179656 | tf_op jit(solution)/shard_map/ppermute | solution.py:521
  59.5 12.4 %collective-permute-start = (bf16[256,384]{1,0:T(8,128)(2,1)S(1)}, bf16[256,384]{1,0:T(8,128)(2,1)S(1)}, u32[]{:S(2)}, u32[]{:S(2)}) collective-permute-start(bf16[256,384]{1,0:T(8,128)(2,1)S(1)} %weight_piece.1.order_ref), channel_id=1, source_target_pairs={{0,64},{1,65},{2,66},{3,67},{4,68},{5,69},{6,70},{7,71},{8,72},{9,... | collective-permute-start | bytes 589832 | tf_op jit(solution)/shard_map/ppermute | solution.py:531
  61.9 9.9 %collective-permute-start.1 = (bf16[256,384]{1,0:T(8,128)(2,1)S(1)}, bf16[256,384]{1,0:T(8,128)(2,1)S(1)}, u32[]{:S(2)}, u32[]{:S(2)}) collective-permute-start(bf16[256,384]{1,0:T(8,128)(2,1)S(1)} %weight_piece.1.order_ref), channel_id=1, source_target_pairs={{0,8},{1,9},{2,10},{3,11},{4,12},{5,13},{6,14},{7,15},{8,64},{9,65... | collective-permute-start | bytes 589832 | tf_op jit(solution)/shard_map/ppermute | solution.py:531
  79.2 30.0 %all-to-all-start.2 = ((bf16[16,128,128]{2,1,0:T(8,128)(2,1)}), bf16[16,128,128]{2,1,0:T(8,128)(2,1)S(1)}, u32[]{:S(2)}, u32[]{:S(2)}) async-start(bf16[16,128,128]{2,1,0:T(8,128)(2,1)} %mix.1.mixed_ref), calls=%async_computation.2 | async-start | bytes 1048576 | tf_op jit(solution)/shard_map/all_to_all | solution.py:609
  89.5 8.4 %collective-permute-start.5 = (bf16[2,256,384]{2,1,0:T(8,128)(2,1)S(1)}, bf16[2,256,384]{2,1,0:T(8,128)(2,1)S(1)}, u32[]{:S(2)}, u32[]{:S(2)}) collective-permute-start(bf16[2,256,384]{2,1,0:T(8,128)(2,1)S(1)} %copy-done.7), channel_id=1, source_target_pairs={{0,48},{16,0},{32,16},{48,32},{64,112},{80,64},{96,80},{112,96},{1... | collective-permute-start | bytes 1179656 | tf_op jit(solution)/shard_map/ppermute | solution.py:521
  91.0 9.7 %collective-permute-start.8 = (bf16[2,256,384]{2,1,0:T(8,128)(2,1)S(1)}, bf16[2,256,384]{2,1,0:T(8,128)(2,1)S(1)}, u32[]{:S(2)}, u32[]{:S(2)}) collective-permute-start(bf16[2,256,384]{2,1,0:T(8,128)(2,1)S(1)} %copy-done.7), channel_id=1, source_target_pairs={{0,16},{16,32},{32,48},{48,0},{64,80},{80,96},{96,112},{112,64},{1... | collective-permute-start | bytes 1179656 | tf_op jit(solution)/shard_map/ppermute | solution.py:521
  100.4 8.7 %collective-permute-start.6 = (bf16[2,256,384]{2,1,0:T(8,128)(2,1)}, bf16[2,256,384]{2,1,0:T(8,128)(2,1)}, u32[]{:S(2)}, u32[]{:S(2)}) collective-permute-start(bf16[2,256,384]{2,1,0:T(8,128)(2,1)} %copy-done.12), channel_id=1, source_target_pairs={{0,16},{16,32},{32,48},{48,0},{64,80},{80,96},{96,112},{112,64},{1... | collective-permute-start | bytes 1179656 | tf_op jit(solution)/shard_map/ppermute | solution.py:521
  109.2 8.2 %collective-permute-start.9 = (bf16[16,128,128]{2,1,0:T(8,128)(2,1)S(1)}, bf16[16,128,128]{2,1,0:T(8,128)(2,1)S(1)}, u32[]{:S(2)}, u32[]{:S(2)}) collective-permute-start(bf16[16,128,128]{2,1,0:T(8,128)(2,1)S(1)} %hold.1.own_ref), channel_id=1, source_target_pairs={{0,128},{128,0},{1,129},{129,1},{2,130},{130,2},{3,131},{131,3},{4... | collective-permute-start | bytes 1572872 | tf_op jit(solution)/shard_map/ppermute | solution.py:516
  125.3 20.6 %all-to-all-start.3 = ((bf16[16,128,128]{2,1,0:T(8,128)(2,1)}), bf16[16,128,128]{2,1,0:T(8,128)(2,1)S(1)}, u32[]{:S(2)}, u32[]{:S(2)}) async-start(bf16[16,128,128]{2,1,0:T(8,128)(2,1)} %add_after.1), calls=%async_computation.3 | async-start | bytes 1048576 | tf_op jit(solution)/shard_map/all_to_all | solution.py:609
  132.7 27.3 %collective-permute-start.12 = (bf16[2,256,384]{2,1,0:T(8,128)(2,1)S(1)}, bf16[2,256,384]{2,1,0:T(8,128)(2,1)S(1)}, u32[]{:S(2)}, u32[]{:S(2)}) collective-permute-start(bf16[2,256,384]{2,1,0:T(8,128)(2,1)S(1)} %copy-done.14), channel_id=1, source_target_pairs={{0,16},{16,32},{32,48},{48,0},{64,80},{80,96},{96,112},{112,64},{1... | collective-permute-start | bytes 1179656 | tf_op jit(solution)/shard_map/ppermute | solution.py:521
  132.8 27.2 %collective-permute-start.13 = (bf16[2,256,384]{2,1,0:T(8,128)(2,1)}, bf16[2,256,384]{2,1,0:T(8,128)(2,1)S(1)}, u32[]{:S(2)}, u32[]{:S(2)}) collective-permute-start(bf16[2,256,384]{2,1,0:T(8,128)(2,1)} %get-tuple-element.36), channel_id=1, source_target_pairs={{0,48},{16,0},{32,16},{48,32},{64,112},{80,64},{96,80},{112,96},{1... | collective-permute-start | bytes 1179656 | tf_op jit(solution)/shard_map/ppermute | solution.py:521
  135.4 24.6 %collective-permute-start.14 = (bf16[2,256,384]{2,1,0:T(8,128)(2,1)}, bf16[2,256,384]{2,1,0:T(8,128)(2,1)}, u32[]{:S(2)}, u32[]{:S(2)}) collective-permute-start(bf16[2,256,384]{2,1,0:T(8,128)(2,1)} %get-tuple-element.37), channel_id=1, source_target_pairs={{0,16},{16,32},{32,48},{48,0},{64,80},{80,96},{96,112},{112,64},{1... | collective-permute-start | bytes 1179656 | tf_op jit(solution)/shard_map/ppermute | solution.py:521
  135.4 24.6 %collective-permute-start.15 = (bf16[2,256,384]{2,1,0:T(8,128)(2,1)}, bf16[2,256,384]{2,1,0:T(8,128)(2,1)}, u32[]{:S(2)}, u32[]{:S(2)}) collective-permute-start(bf16[2,256,384]{2,1,0:T(8,128)(2,1)} %get-tuple-element.38), channel_id=1, source_target_pairs={{0,48},{16,0},{32,16},{48,32},{64,112},{80,64},{96,80},{112,96},{1... | collective-permute-start | bytes 1179656 | tf_op jit(solution)/shard_map/ppermute | solution.py:521
  153.2 43.0 %all-to-all-start.4 = ((bf16[16,128,128]{2,1,0:T(8,128)(2,1)}), bf16[16,128,128]{2,1,0:T(8,128)(2,1)S(1)}, u32[]{:S(2)}, u32[]{:S(2)}) async-start(bf16[16,128,128]{2,1,0:T(8,128)(2,1)} %grad_of_value.1.order_ref.refs_8_), calls=%async_computation.4 | async-start | bytes 1048576 | tf_op jit(solution)/shard_map/all_to_all | solution.py:609
  164.2 10.8 %collective-permute-start.16 = (bf16[2,256,384]{2,1,0:T(8,128)(2,1)}, bf16[2,256,384]{2,1,0:T(8,128)(2,1)S(1)}, u32[]{:S(2)}, u32[]{:S(2)}) collective-permute-start(bf16[2,256,384]{2,1,0:T(8,128)(2,1)} %get-tuple-element.40), channel_id=1, source_target_pairs={{0,16},{16,32},{32,48},{48,0},{64,80},{80,96},{96,112},{112,64},{1... | collective-permute-start | bytes 1179656 | tf_op jit(solution)/shard_map/ppermute | solution.py:521
  164.3 10.8 %collective-permute-start.17 = (bf16[2,256,384]{2,1,0:T(8,128)(2,1)}, bf16[2,256,384]{2,1,0:T(8,128)(2,1)S(1)}, u32[]{:S(2)}, u32[]{:S(2)}) collective-permute-start(bf16[2,256,384]{2,1,0:T(8,128)(2,1)} %get-tuple-element.42), channel_id=1, source_target_pairs={{0,48},{16,0},{32,16},{48,32},{64,112},{80,64},{96,80},{112,96},{1... | collective-permute-start | bytes 1179656 | tf_op jit(solution)/shard_map/ppermute | solution.py:521
  167.2 25.1 %collective-permute-start.10 = (bf16[128,768]{1,0:T(8,128)(2,1)S(1)}, bf16[128,768]{1,0:T(8,128)(2,1)S(1)}, u32[]{:S(2)}, u32[]{:S(2)}) collective-permute-start(bf16[128,768]{1,0:T(8,128)(2,1)S(1)} %copy-done.21), channel_id=1, source_target_pairs={{0,128},{128,0},{1,129},{129,1},{2,130},{130,2},{3,131},{131,3},{4... | collective-permute-start | bytes 589832 | tf_op jit(solution)/shard_map/ppermute | solution.py:516
  178.5 16.3 %collective-permute-start.18 = (bf16[256,384]{1,0:T(8,128)(2,1)}, bf16[256,384]{1,0:T(8,128)(2,1)S(1)}, u32[]{:S(2)}, u32[]{:S(2)}) collective-permute-start(bf16[256,384]{1,0:T(8,128)(2,1)} %get-tuple-element.44), channel_id=1, source_target_pairs={{0,8},{1,9},{2,10},{3,11},{4,12},{5,13},{6,14},{7,15},{8,64},{9,65... | collective-permute-start | bytes 589832 | tf_op jit(solution)/shard_map/ppermute | solution.py:531
  179.6 15.3 %collective-permute-start.19 = (bf16[256,384]{1,0:T(8,128)(2,1)}, bf16[256,384]{1,0:T(8,128)(2,1)S(1)}, u32[]{:S(2)}, u32[]{:S(2)}) collective-permute-start(bf16[256,384]{1,0:T(8,128)(2,1)} %get-tuple-element.45), channel_id=1, source_target_pairs={{0,72},{1,73},{2,74},{3,75},{4,76},{5,77},{6,78},{7,79},{8,0},{9,1... | collective-permute-start | bytes 589832 | tf_op jit(solution)/shard_map/ppermute | solution.py:531
  181.9 14.3 %collective-permute-start.20 = (bf16[256,384]{1,0:T(8,128)(2,1)}, bf16[256,384]{1,0:T(8,128)(2,1)}, u32[]{:S(2)}, u32[]{:S(2)}) collective-permute-start(bf16[256,384]{1,0:T(8,128)(2,1)} %get-tuple-element.46), channel_id=1, source_target_pairs={{0,64},{1,65},{2,66},{3,67},{4,68},{5,69},{6,70},{7,71},{8,72},{9,... | collective-permute-start | bytes 589832 | tf_op jit(solution)/shard_map/ppermute | solution.py:531
  231.7 8.1 %collective-permute-start.21 = (f32[16,768]{1,0:T(8,128)S(1)}, f32[16,768]{1,0:T(8,128)S(1)}, u32[]{:S(2)}, u32[]{:S(2)}) collective-permute-start(f32[16,768]{1,0:T(8,128)S(1)} %sum_extra.1.own_ref.order_ref), channel_id=1, source_target_pairs={{0,128},{128,0},{1,129},{129,1},{2,130},{130,2},{3,131},{131,3},{4... | collective-permute-start | bytes 147464 | tf_op jit(solution)/shard_map/ppermute | solution.py:516
  (27 other events, 336.1 us)
